TPU v7x, 32 devices: a whole 2x2x4 slice. The times are simulated.
32 devices in a mesh: batch: 4 (over y, x), strip: 8 (over z, core).
Axes of the slice: x: 2, y: 2, z: 4, core: 2. Of those that a mesh axis runs over, the one named last changes fastest.
Arguments:
- tokens: bfloat16 [4, 64, 32, 768], P('batch', 'strip'), may hold values from -6 to 6
- tile_owner: int32 [4, 4, 2], P('batch'), may hold values from 0 to 7, as said below
- time_steps: int32 [4, 8], P('batch'), may hold values from 0 to 999
- class_labels: int32 [4, 8], P('batch'), may hold values from 0 to 999
- class_embedding_matrix: bfloat16 [768, 1000], replicated, may hold values from -6 to 6
- adaptive_weight: bfloat16 [768, 4608], replicated, may hold values from -0.21875 to 0.21875
- adaptive_bias: bfloat16 [4608], replicated, may hold values from -3 to 3
- mixer_kernel: bfloat16 [768, 9], replicated, may hold values from -2 to 2
- joint_weight: bfloat16 [768, 2304], replicated, may hold values from -0.21875 to 0.21875
- output_weight: bfloat16 [768, 768], replicated, may hold values from -2.5 to 2.5
- output_bias: bfloat16 [768], replicated, may hold values from -2 to 2
- expand_weight: bfloat16 [768, 3072], replicated, may hold values from -0.21875 to 0.21875
- expand_bias: bfloat16 [3072], replicated, may hold values from -2 to 2
- hidden_kernel: bfloat16 [3072, 9], replicated, may hold values from -2 to 2
- reduce_weight: bfloat16 [3072, 768], replicated, may hold values from -0.109375 to 0.109375
- reduce_bias: bfloat16 [768], replicated, may hold values from -2 to 2
- output_cotangent: bfloat16 [4, 64, 32, 768], P('batch', 'strip'), may hold values from -6 to 6
Outputs:
- outputs: bfloat16 [4, 64, 32, 768], P('batch', 'strip')
- tokens_grad: float32 [4, 64, 32, 768], P('batch', 'strip')
- class_table_grad: float32 [768, 1000], P('strip')
- adaptive_weight_grad: float32 [768, 4608], P('strip')
- adaptive_bias_grad: float32 [4608], P('strip')
- mixer_kernel_grad: float32 [768, 9], P('strip')
- joint_weight_grad: float32 [768, 2304], P('strip')
- output_weight_grad: float32 [768, 768], P('strip')
- output_bias_grad: float32 [768], P('strip')
- expand_weight_grad: float32 [768, 3072], P('strip')
- expand_bias_grad: float32 [3072], P('strip')
- hidden_kernel_grad: float32 [3072, 9], P('strip')
- reduce_weight_grad: float32 [3072, 768], P('strip')
- reduce_bias_grad: float32 [768], P('strip')
Inputs may be any that keep to these rules, and one draw needn't show every extreme that they name: `tile_owner`: A canvas is cut into 4 x 2 tiles of 16 rows and 16 columns; the tiles of one slot form one latent, a rectangle of whole tiles; among the canvases of each index of batch, some canvas has a latent that spans all 64 rows.
All inputs are finite; a program needn't handle non-finite values.
Results may differ from a plain program's by a relative error of at most 0.023.
Values may be sent and summed in bfloat16 or wider, within the bound.
A program may use at most 320 MiB of HBM per device.

v0:
```python
import math
from types import SimpleNamespace

import jax
import jax.numpy as jnp
from jax import lax
from jax.experimental import pallas as pl
from jax.experimental.pallas import tpu as pltpu
from jax.sharding import PartitionSpec as P

HEADS = 12
EPSILON = 1e-06
MASKED = -1e30
MESH = pl.DeviceIdType.MESH
F32 = jnp.float32
BF16 = jnp.bfloat16
VMEM_BYTES = 62 * 1024 * 1024
WHOLE = pl.BlockSpec(memory_space=pltpu.VMEM)
LEFT = pl.BlockSpec(memory_space=pl.ANY)
SCALARS = pl.BlockSpec(memory_space=pltpu.SMEM)
NT = (((1,), (1,)), ((), ()))
TN = (((0,), (0,)), ((), ()))


def dot(a, b):
    return jnp.dot(a, b, preferred_element_type=F32)


def dot_nt(a, b):
    return lax.dot_general(a, b, NT, preferred_element_type=F32)


def dot_tn(a, b):
    return lax.dot_general(a, b, TN, preferred_element_type=F32)


def send_to(src, dst, sems, index, batch, strip):
    return pltpu.make_async_remote_copy(
        src_ref=src,
        dst_ref=dst,
        send_sem=sems[0].at[index],
        recv_sem=sems[1].at[index],
        device_id=(batch, strip),
        device_id_type=MESH,
    )


def entry_barrier(strips):
    s = lax.axis_index("strip")
    b = lax.axis_index("batch")
    z = s // 2
    barrier = pltpu.get_barrier_semaphore()
    count = 0
    for d in range(1, strips):
        pl.semaphore_signal(
            barrier, inc=1, device_id=(b, lax.rem(s + d, strips)), device_id_type=MESH
        )
        count += 1
    for e in range(1, 4):
        for core in range(2):
            pl.semaphore_signal(
                barrier, inc=1, device_id=(lax.rem(b + e, 4), 2 * z + core), device_id_type=MESH
            )
            count += 1
    pl.semaphore_wait(barrier, count)


def spread(mod, width):
    return jnp.concatenate(
        [jnp.broadcast_to(mod[0:1], (8, width)), jnp.broadcast_to(mod[1:2], (8, width))], axis=0
    )


def spread_columns(buffer, r, x):
    for k in range(x.shape[-1] // 128):
        buffer[r, k] = x[:, k * 128 : k * 128 + 128]


def every_second(buffer, r, p):
    return jnp.concatenate(
        [buffer[r, k, pl.ds(p, 16, stride=2), :] for k in range(buffer.shape[1])], axis=-1
    )


def interleave(buffer, r, p, x):
    for k in range(x.shape[-1] // 128):
        buffer[r, k, pl.ds(p, 16, stride=2), :] = x[:, k * 128 : k * 128 + 128]


def joined(buffer, r):
    return jnp.concatenate([buffer[r, k] for k in range(buffer.shape[1])], axis=-1)


def ln_parts(x):
    centre = jnp.mean(x, axis=-1, keepdims=True)
    centred = x - centre
    var = jnp.mean(centred * centred, axis=-1, keepdims=True)
    inv = lax.rsqrt(var + EPSILON)
    return centred * inv, inv


def ln_back(grad, n, inv):
    mean0 = jnp.mean(grad, axis=-1, keepdims=True)
    mean1 = jnp.mean(grad * n, axis=-1, keepdims=True)
    return inv * (grad - mean0 - n * mean1)


def window(load, r):
    even = load(r, 0).astype(F32)
    odd = load(r, 1).astype(F32)
    n = even.shape[0]
    j = lax.broadcasted_iota(jnp.int32, even.shape, 0)
    odd_m = jnp.where(j == 0, 0.0, pltpu.roll(odd, 1, 0))
    even_p = jnp.where(j == n - 1, 0.0, pltpu.roll(even, n - 1, 0))
    return odd_m, even, odd, even_p


def conv(rows, weights, flip):
    out = []
    for p in range(2):
        total = None
        for i in range(3):
            for j in range(3):
                t = 3 * i + j
                a = weights[8 - t if flip else t] * rows[i][p + j]
                total = a if total is None else total + a
        out.append(total)
    return out


def taps(rows, centre, sums):
    new = list(sums)
    for i in range(3):
        for j in range(3):
            a = rows[i][j] * centre[0] + rows[i][1 + j] * centre[1]
            t = 8 - (3 * i + j)
            new[t] = sums[t] + (a[0:8] + a[8:16])
    return new


def halves(x):
    return jnp.concatenate(
        [jnp.sum(x[0:8], axis=0, keepdims=True), jnp.sum(x[8:16], axis=0, keepdims=True)], axis=0
    )


def gelu_both(x):
    k0 = math.sqrt(2.0 / math.pi)
    square = x * x
    t = jnp.tanh(k0 * x * (1.0 + 0.044715 * square))
    cdf = 0.5 + 0.5 * t
    slope = cdf + (0.5 * k0) * x * (1.0 - t * t) * (1.0 + (3.0 * 0.044715) * square)
    return x * cdf, slope


def condition_kernel(owner, steps, labels, emb, ab, aw_hbm, mod_ref, cond_ref, aw, sem):
    s = lax.axis_index("strip")
    b = lax.axis_index("batch")
    z = s // 2
    classes, width = emb.shape
    latents = steps.shape[1]
    half = width // 2
    copies = []
    for i in range(6):
        cp = pltpu.make_async_copy(aw_hbm.at[:, pl.ds(i * width, width)], aw.at[i], sem.at[i])
        cp.start()
        copies.append(cp)

    row = lax.broadcasted_iota(jnp.int32, (latents, 1), 0)
    when = jnp.zeros((latents, 1), F32)
    label = jnp.zeros((latents, 1), jnp.int32)
    for i in range(latents):
        when = jnp.where(row == i, steps[0, i].astype(F32), when)
        label = jnp.where(row == i, labels[0, i], label)
    order = lax.broadcasted_iota(jnp.int32, (latents, half), 1).astype(F32)
    angles = when * jnp.exp(-math.log(10000.0) * order / half)
    features = jnp.concatenate([jnp.cos(angles), jnp.sin(angles)], axis=1)
    onehot = lax.broadcasted_iota(jnp.int32, (latents, classes), 1) == label
    condition = features + dot(jnp.where(onehot, 1.0, 0.0).astype(BF16), emb[...])
    silu = (condition / (1.0 + jnp.exp(-condition))).astype(BF16)

    lane = lax.broadcasted_iota(jnp.int32, (latents, 128), 1)
    kind = lax.broadcasted_iota(jnp.int32, (latents, 128), 0)
    line = lax.rem(lane, 16)
    side = jnp.where(kind == 0, lax.rem(line // 2, 2), lax.rem(line // 3, 2))
    tile = lax.rem(lane // 16, 4)
    slots = jnp.zeros((latents, 128), jnp.int32)
    for i in range(4):
        for h in range(2):
            hit = jnp.logical_and(tile == i, side == h)
            slots = jnp.where(hit, owner[0, h, i] + b * latents, slots)
    cond_ref[...] = jnp.concatenate(
        [condition, jnp.broadcast_to(label.astype(F32), (latents, 128)), slots.astype(F32)], axis=1
    )

    bias = ab[...].astype(F32).reshape(1, 6 * width)
    for i in range(6):
        copies[i].wait()
        lanes = slice(i * width, i * width + width)
        table = dot(silu, aw[i]) + bias[:, lanes]
        for h in range(2):
            mine = row == owner[0, h, z]
            mod_ref[h : h + 1, lanes] = jnp.sum(
                jnp.where(mine, table, 0.0), axis=0, keepdims=True
            )


def conditioning(owner, steps, labels, emb, ab, aw):
    width = emb.shape[1]
    latents = steps.shape[1]
    shape = jax.ShapeDtypeStruct
    return pl.pallas_call(
        condition_kernel,
        name="conditioning",
        out_shape=(shape((2, 6 * width), F32), shape((latents, width + 256), F32)),
        in_specs=[SCALARS] * 3 + [WHOLE] * 2 + [LEFT],
        out_specs=(WHOLE, WHOLE),
        scratch_shapes=[pltpu.VMEM((6, width, width), BF16), pltpu.SemaphoreType.DMA((6,))],
        compiler_params=pltpu.CompilerParams(vmem_limit_bytes=VMEM_BYTES),
    )(owner, steps, labels, emb, ab, aw)


def block_kernel(names, *refs):
    m = SimpleNamespace(**dict(zip(names, refs)))
    rows, cols, width = m.tok.shape
    half = width // 2
    strips = lax.axis_size("strip")
    chips = strips // 2
    chip_rows = 2 * rows
    total = strips * 64
    own = width // strips
    s = lax.axis_index("strip")
    b = lax.axis_index("batch")
    z = s // 2
    c = lax.rem(s, 2)
    sibling = 2 * z + 1 - c
    y, x = b // 2, lax.rem(b, 2)
    x_mate = 2 * y + 1 - x
    y_mate = 2 * (1 - y) + x
    sent = []

    def chip(d):
        return lax.rem(z + d, chips)

    def start(copy):
        copy.start()
        sent.append(copy)

    loads = {}

    def load(name, src, dst, index):
        loads[name] = pltpu.make_async_copy(src, dst, m.load_sem.at[index])
        loads[name].start()

    for part in range(3):
        off = pl.multiple_of(part * width + c * half, 128)
        load(f"wj{part}", m.wj_hbm.at[:, pl.ds(off, half)], m.wj.at[part], part)
    load("cot", m.cot_hbm, m.cot, 3)
    load("wo", m.wo_hbm, m.wo, 4)
    for n in range(chips):
        off = pl.multiple_of((2 * n + c) * half, 128)
        spot = pl.ds(n * half, half)
        load(f"we{n}", m.we_hbm.at[:, pl.ds(off, half)], m.we.at[:, spot], 5 + n)
        load(f"wr{n}", m.wr_hbm.at[pl.ds(off, half)], m.wr.at[spot], 5 + chips + n)
    entry_barrier(strips)

    m.mk[...] = m.mixer[...].astype(F32)
    ob = m.ob[...].astype(F32).reshape(1, width)
    rb = m.rb[...].astype(F32).reshape(1, width)
    m.ebf[...] = m.eb[...].astype(F32).reshape(m.ebf.shape)
    for n in range(chips):
        m.hk[n] = m.hidden[:, pl.ds(pl.multiple_of((2 * n + c) * half, 128), half)].astype(F32)

    m.cond_all[b] = m.cond[...]
    for e in range(1, 4):
        start(
            send_to(m.cond_all.at[b], m.cond_all.at[b], m.cond_sem, e, lax.rem(b + e, 4), s)
        )

    def block_mod(n):
        return spread(m.mod[:, n * width : (n + 1) * width], width)

    scale1 = 1.0 + block_mod(1)
    shift1 = block_mod(0)

    def first_row(r):
        spread_columns(m.rowf, r, m.tok[r].astype(F32))
        for p in range(2):
            v = every_second(m.rowf, r, p)
            m.xd[r, p] = v.astype(BF16)
            n, _ = ln_parts(v)
            m.fp[r + 1, p] = (n * scale1 + shift1).astype(BF16)

    def edge_sends(buffer, sems):
        up = send_to(buffer.at[1], buffer.at[rows + 1], sems, 0, b, s - 1)
        down = send_to(buffer.at[rows], buffer.at[0], sems, 1, b, s + 1)
        return up, down

    def start_edges(buffer, sems):
        up, down = edge_sends(buffer, sems)

        @pl.when(s > 0)
        def _():
            up.start()

        @pl.when(s < strips - 1)
        def _():
            down.start()

    def edges_sent(buffer, sems):
        up, down = edge_sends(buffer, sems)

        @pl.when(s > 0)
        def _():
            up.wait_send()

        @pl.when(s < strips - 1)
        def _():
            down.wait_send()

    def top_edge(buffer, sems):
        @pl.when(s > 0)
        def _():
            send_to(buffer.at[1], buffer.at[0], sems, 1, b, s - 1).wait_recv()

        @pl.when(s == 0)
        def _():
            buffer[0] = jnp.zeros_like(buffer[0])

    def bottom_edge(buffer, sems):
        @pl.when(s < strips - 1)
        def _():
            send_to(buffer.at[1], buffer.at[rows + 1], sems, 0, b, s + 1).wait_recv()

        @pl.when(s == strips - 1)
        def _():
            buffer[rows + 1] = jnp.zeros_like(buffer[0])

    first_row(0)
    first_row(rows - 1)
    start_edges(m.fp, m.fp_sem)

    def body(r, _):
        first_row(r)
        return 0

    lax.fori_loop(1, rows - 1, body, 0, unroll=3)

    def mixed_rows(low, high):
        for k in range(width // 128):
            lanes = pl.ds(k * 128, 128)
            weights = [m.mk[t : t + 1, k * 128 : k * 128 + 128] for t in range(9)]

            def line(r, p):
                return m.fp[r, p, :, lanes]

            def step(r, carry):
                new = window(line, r + 2)
                out = conv((carry[0], carry[1], new), weights, False)
                for p in range(2):
                    m.ms[lax.rem(r, 2) * 2 + p, r // 2, :, lanes] = out[p].astype(BF16)
                return carry[1], new

            lax.fori_loop(
                low, high, step, (window(line, low), window(line, low + 1)), unroll=True
            )

    mixed_rows(1, rows - 1)
    top_edge(m.fp, m.fp_sem)
    mixed_rows(0, 1)
    bottom_edge(m.fp, m.fp_sem)
    mixed_rows(rows - 1, rows)

    def to_groups(source, target, sems, sems2):
        for d in range(1, chips):
            g = chip(d)
            start(send_to(source.at[g], target.at[s], sems, d, b, 2 * g + c))
        target[s] = source[z]

    def pass_on(target, sems, sems2, d):
        i = 2 * chip(chips - d) + c
        if d:
            send_to(target.at[i], target.at[i], sems, d, b, i).wait_recv()
        start(send_to(target.at[i], target.at[i], sems2, d, b, sibling))

    def groups_ready(target, sems2):
        for d in range(chips):
            i = 2 * chip(chips - d) + 1 - c
            send_to(target.at[i], target.at[i], sems2, d, b, sibling).wait_recv()

    to_groups(m.ms, m.mg, m.mg_sem, m.mg_sem2)

    m.acc[...] = jnp.zeros_like(m.acc)
    gate2 = block_mod(5)
    loads["cot"].wait()

    def upstream_row(r, _):
        spread_columns(m.rowf, r, m.cot[r].astype(F32))
        for p in range(2):
            up = every_second(m.rowf, r, p)
            m.ctd[2 * r + p] = up.astype(BF16)
            two = (up * gate2).astype(BF16)
            m.tg[c, 2 * r + p] = two
            m.acc[0] += two.astype(F32)
        return 0

    lax.fori_loop(0, rows, upstream_row, 0)
    start(send_to(m.tg.at[c], m.tg.at[c], m.pair_sem, 0, b, sibling))

    for d in range(chips):
        pass_on(m.mg, m.mg_sem, m.mg_sem2, d)
    groups_ready(m.mg, m.mg_sem2)
    for part in range(3):
        loads[f"wj{part}"].wait()

    v = m.mg[...].reshape(total, width)
    for part in range(3):
        w = dot(v, m.wj[part]).astype(BF16)
        for n in range(3):
            m.qkv[3 * part + n] = w[:, n * 128 : n * 128 + 128]

    where = lax.broadcasted_iota(jnp.int32, (1, total), 1)
    lefts = lax.rem(where, 16) < 8
    key_owner = jnp.zeros((1, total), jnp.int32)
    for t in range(4):
        both = jnp.where(lefts, m.owner[0, 0, t], m.owner[0, 1, t])
        key_owner = jnp.where(where // 128 == t, both, key_owner)
    where = lax.broadcasted_iota(jnp.int32, (total, 1), 0)
    lefts = lax.rem(where, 16) < 8
    query_owner = jnp.zeros((total, 1), jnp.int32)
    for t in range(4):
        both = jnp.where(lefts, m.owner[0, 0, t], m.owner[0, 1, t])
        query_owner = jnp.where(where // 128 == t, both, query_owner)
    allowed = query_owner == key_owner
    lane = lax.broadcasted_iota(jnp.int32, (total, 128), 1) < 64
    factor = 64 ** -0.5

    def head(v, h):
        return jnp.where(lane if h == 0 else jnp.logical_not(lane), v, jnp.zeros_like(v))

    for n in range(3):
        mine = c * 3 + n
        q2 = (m.qkv[n].astype(F32) * factor).astype(BF16)
        outs = []
        for h in range(2):
            scores = jnp.where(allowed, dot_nt(head(q2, h), m.qkv[3 + n]), MASKED)
            peak = jnp.max(scores, axis=-1, keepdims=True)
            lifted = jnp.exp(scores - peak)
            inv = 1.0 / jnp.sum(lifted, axis=-1, keepdims=True)
            m.probs[n, h] = (lifted * inv).astype(BF16)
            outs.append(dot(lifted.astype(BF16), m.qkv[6 + n]) * inv)
        m.ag[mine] = jnp.where(lane, outs[0], outs[1]).astype(BF16)
        for d in range(1, strips):
            t = lax.rem(s + d, strips)
            start(
                send_to(
                    m.ag.at[mine, pl.ds(pl.multiple_of(t * 64, 64), 64)],
                    m.ai.at[mine, z],
                    m.ai_sem,
                    (n, d),
                    b,
                    t,
                )
            )
        start(send_to(m.ag.at[mine], m.ag.at[mine], m.ag_sem, n, b, sibling))
        m.ai[mine, z] = m.ag[mine, pl.ds(pl.multiple_of(s * 64, 64), 64), :]

    for n in range(3):
        for d in range(1, strips):
            i = lax.rem(s - d + strips, strips)
            spot = lax.rem(i, 2) * 3 + n
            send_to(
                m.ag.at[spot, pl.ds(0, 64)], m.ai.at[spot, i // 2], m.ai_sem, (n, d), b, i
            ).wait_recv()

    gate1 = block_mod(2)
    shift2 = block_mod(3)
    scale2 = 1.0 + block_mod(4)
    loads["wo"].wait()

    v = jnp.concatenate([m.ai[n].reshape(chips * 64, 128) for n in range(6)], axis=-1)
    m.b1[...] = (dot(v, m.wo[...]) + ob).reshape(m.b1.shape)

    def residual_row(i, _):
        rp = 4 * lax.rem(i, rows // 2) + i // (rows // 2)
        u = m.xd[rp // 2, lax.rem(rp, 2)].astype(F32) + gate1 * m.b1[i]
        m.res[rp] = u
        n, _ = ln_parts(u)
        m.sc[c, rp] = (n * scale2 + shift2).astype(BF16)
        return 0

    lax.fori_loop(0, 2 * rows, residual_row, 0, unroll=4)
    start(send_to(m.sc.at[c], m.sc.at[c], m.pair_sem, 1, b, sibling))

    def halo_sends(buffer, sems):
        up = send_to(buffer.at[1], buffer.at[chip_rows + 1], sems, 0, b, s - 2)
        down = send_to(buffer.at[chip_rows], buffer.at[0], sems, 1, b, s + 2)
        return up, down

    def start_halo(buffer, sems, upward, downward):
        up, down = halo_sends(buffer, sems)

        @pl.when(jnp.logical_and(z > 0, upward))
        def _():
            up.start()

        @pl.when(jnp.logical_and(z < chips - 1, downward))
        def _():
            down.start()

    def halo_sent(buffer, sems):
        up, down = halo_sends(buffer, sems)

        @pl.when(z > 0)
        def _():
            up.wait_send()

        @pl.when(z < chips - 1)
        def _():
            down.wait_send()

    def take_halo(buffer, sems):
        @pl.when(z > 0)
        def _():
            send_to(buffer.at[1], buffer.at[0], sems, 1, b, s - 2).wait_recv()

        @pl.when(z == 0)
        def _():
            buffer[0] = jnp.zeros_like(buffer[0])

        @pl.when(z < chips - 1)
        def _():
            send_to(buffer.at[1], buffer.at[chip_rows + 1], sems, 0, b, s + 2).wait_recv()

        @pl.when(z == chips - 1)
        def _():
            buffer[chip_rows + 1] = jnp.zeros_like(buffer[0])

    for n in range(chips):
        loads[f"we{n}"].wait()
        loads[f"wr{n}"].wait()
    hidden = chips * half
    bias = jnp.concatenate(
        [m.ebf[:, pl.ds(pl.multiple_of((2 * n + c) * half, 128), half)] for n in range(chips)],
        axis=-1,
    )

    def expand(core):
        w = dot(m.sc[core].reshape(rows * 32, width), m.we[...]) + bias
        m.ex[pl.ds(1 + core * rows, rows)] = w.astype(BF16).reshape(rows, 2, 16, hidden)

    expand(c)
    start_halo(m.ex, m.ex_sem, c == 0, c == 1)
    send_to(m.sc.at[c], m.sc.at[1 - c], m.pair_sem, 1, b, sibling).wait_recv()
    expand(1 - c)
    start_halo(m.ex, m.ex_sem, c == 1, c == 0)
    send_to(m.tg.at[c], m.tg.at[1 - c], m.pair_sem, 0, b, sibling).wait_recv()
    chip_tg = m.tg[...].reshape(total, width)
    for h in range(2):
        m.big[h] = dot_nt(chip_tg, m.wr[h * width : h * width + width, :]).reshape(m.big.shape[1:])

    first_mate, then_mate = (x_mate, y_mate), (y_mate, x_mate)
    part_rows = width // 8

    def r_source(n, h, mine):
        at = pl.ds(h * part_rows, part_rows)
        if h == 0:
            return m.rw.at[n, :, x if mine else 1 - x, at]
        return m.rw.at[n, y if mine else 1 - y, :, at]

    def r_one(n, h):
        return send_to(r_source(n, h, False), m.r1.at[n, h], m.r1_sem, (n, h), first_mate[h], s)

    def r_two(n, h):
        src = m.r1.at[n, h, (1 - y) if h == 0 else (1 - x)]
        return send_to(src, m.r2.at[n, h], m.r2_sem, (n, h), then_mate[h], s)

    def r_three(k):
        z_pair = z + 1 - 2 * lax.rem(z, 2)
        z_far = lax.rem(z + 2, 4)
        dest = z_pair if k < 2 else z_far
        t = (z_pair, 3 - z, z_far)[k]
        return send_to(m.r2.at[t], m.r3.at[k], m.r3_sem, k, b, 2 * dest + c)

    def r_four(e):
        return send_to(m.r_all.at[b], m.r_all.at[b], m.r4_sem, e, lax.rem(b + e, 4), s)

    def r_half(n):
        for h in range(2):
            r_one(n, h).wait_recv()
            kept = r_source(n, h, True)[...].astype(F32)
            m.r1[n, h] = (m.r1[n, h].astype(F32) + kept).astype(BF16)
            r_two(n, h).start()

    def r_quarter(n):
        for h in range(2):
            r_two(n, h).wait_recv()
            kept = m.r1[n, h, y if h == 0 else x].astype(F32)
            m.r2[n, h] = (m.r2[n, h].astype(F32) + kept).astype(BF16)

    def r_spread():
        r_three(1).start()
        r_three(0).start()

    def r_across():
        r_three(1).wait_recv()
        t = lax.rem(z + 2, 4)
        m.r2[t] = (m.r2[t].astype(F32) + m.r3[1].astype(F32)).astype(BF16)
        r_three(2).start()

    def r_sum():
        v = m.r2[z].astype(F32)
        for k in (0, 2):
            r_three(k).wait_recv()
            v = v + m.r3[k].astype(F32)
        m.r_all[b] = v.astype(BF16)
        for e in range(1, 4):
            r_four(e).start()

    def c_source(j, h, mine):
        block = m.ew.at[j] if not isinstance(j, int) or j < 4 else m.jo.at[j - 4]
        at = pl.ds(2 * h, 2)
        if h == 0:
            return block.at[at, :, x if mine else 1 - x]
        return block.at[at, y if mine else 1 - y]

    def c_one(j, h):
        return send_to(c_source(j, h, False), m.c1.at[j, h], m.c1_sem, (j, h), first_mate[h], s)

    def c_two(j, h):
        src = m.c1.at[j, h, :, 1 - y] if h == 0 else m.c1.at[j, h, :, 1 - x]
        return send_to(src, m.c2.at[j, pl.ds(2 * h, 2)], m.c2_sem, (j, h), then_mate[h], s)

    pair_chip = z + 1 - 2 * lax.rem(z, 2)
    far_chip = lax.rem(z + 2, 4)
    last_chip = 3 - z

    def c_three(j, k):
        dest = pair_chip if k < 2 else far_chip
        t = (pair_chip, last_chip, far_chip)[k]
        return send_to(m.c2.at[j, t], m.c3.at[j, k], m.c3_sem, (j, k), b, 2 * dest + c)

    def c_four(j, e):
        return pltpu.make_async_remote_copy(
            src_ref=m.c_out.at[j],
            dst_ref=m.c_all.at[j, x, c],
            send_sem=m.c4_sem[0].at[j, e],
            recv_sem=m.c4_sem[1].at[j, e, c],
            device_id=(lax.rem(b + e, 4), 2 * z + y),
            device_id_type=MESH,
        )

    def c_begin(j):
        for h in range(2):
            c_one(j, h).start()

    def c_half(j):
        for h in range(2):
            c_one(j, h).wait_recv()
            kept = c_source(j, h, True)[...].astype(F32)
            m.c1[j, h] = (m.c1[j, h].astype(F32) + kept).astype(BF16)
            c_two(j, h).start()

    def c_quarter(j):
        for h in range(2):
            c_two(j, h).wait_recv()
            at = pl.ds(2 * h, 2)
            kept = (m.c1[j, h, :, y] if h == 0 else m.c1[j, h, :, x]).astype(F32)
            m.c2[j, at] = (m.c2[j, at].astype(F32) + kept).astype(BF16)

    def c_spread(j):
        c_three(j, 1).start()
        c_three(j, 0).start()

    def c_across(j):
        c_three(j, 1).wait_recv()
        far = m.c2[j, far_chip].astype(F32) + m.c3[j, 1].astype(F32)
        m.c2[j, far_chip] = far.astype(BF16)
        c_three(j, 2).start()

    def c_sum(j):
        v = m.c2[j, z].astype(F32)
        for k in (0, 2):
            c_three(j, k).wait_recv()
            v = v + m.c3[j, k].astype(F32)
        m.c_out[j] = v.astype(BF16)

        @pl.when(c == y)
        def _():
            m.c_all[j, x, c] = m.c_out[j]

        for e in range(1, 4):
            c_four(j, e).start()

        @pl.when(c != y)
        def _():
            c_four(j, 0).start()

    take_halo(m.ex, m.ex_sem)

    def activate(n, _):
        for k in range(3):
            lanes = pl.ds(pl.multiple_of(n * half + k * 128, 128), 128)
            inner = pl.ds(k * 128, 128)
            weights = [m.hk[n, t : t + 1, inner] for t in range(9)]
            spot = pl.ds(pl.multiple_of(lax.rem(n, 2) * half + k * 128, 128), 128)

            def line(r, p):
                return m.ex[r, p, :, lanes]

            above, here = window(line, 0), window(line, 1)
            for r in range(chip_rows):
                below = window(line, r + 2)
                out = conv((above, here, below), weights, False)
                for p in range(2):
                    value, slope = gelu_both(out[p])
                    rp = 2 * r + p
                    grad = m.big[n // 2, rp // 16, rp % 16, :, spot]
                    m.act[rp, :, lanes] = value.astype(BF16)
                    m.cg[r + 1, p, :, lanes] = (grad * slope).astype(BF16)
                above, here = here, below
        full = m.act[:, :, pl.ds(pl.multiple_of(n * half, 128), half)].reshape(total, half)
        m.rw[n] = dot_tn(chip_tg, full).astype(BF16).reshape(m.rw.shape[1:])
        for h in range(2):
            r_one(n, h).start()
        return 0

    lax.fori_loop(0, chips, activate, 0)
    start_halo(m.cg, m.cg_sem, True, True)
    full = m.act[...].reshape(total, hidden)
    m.big[0] = dot(full, m.wr[...]).reshape(m.big.shape[1:])
    b2_copy = send_to(m.big.at[0, 1 - c], m.b2_in, m.pair_sem, 2, b, sibling)
    b2_copy.start()
    m.hkg[...] = jnp.zeros_like(m.hkg)
    take_halo(m.cg, m.cg_sem)
    chip_sc = m.sc[...].reshape(total, width)

    def backward(n, _):
        for k in range(3):
            lanes = pl.ds(pl.multiple_of(n * half + k * 128, 128), 128)
            inner = pl.ds(k * 128, 128)
            weights = [m.hk[n, t : t + 1, inner] for t in range(9)]

            def line(r, p):
                return m.cg[r, p, :, lanes]

            above, here = window(line, 0), window(line, 1)
            sums = [jnp.zeros((8, 128), F32) for _ in range(9)]
            total_eg = jnp.zeros((8, 128), F32)
            for r in range(chip_rows):
                below = window(line, r + 2)
                three = (above, here, below)
                low = [v.astype(BF16) for v in conv(three, weights, True)]
                for p in range(2):
                    m.act[2 * r + p, :, lanes] = low[p]
                centre = [m.ex[r + 1, p, :, lanes].astype(F32) for p in range(2)]
                sums = taps(three, centre, sums)
                both = low[0].astype(F32) + low[1].astype(F32)
                total_eg = total_eg + (both[0:8] + both[8:16])
                above, here = here, below
            for t, v in enumerate(sums + [total_eg]):
                m.hkg[n, t : t + 1, inner] = jnp.sum(v, axis=0, keepdims=True)
        full = m.act[:, :, pl.ds(pl.multiple_of(n * half, 128), half)].reshape(total, half)
        m.ew[n] = dot_tn(chip_sc, full).astype(BF16).reshape(m.ew.shape[1:])
        c_begin(n)
        r_half(n)
        return 0

    lax.fori_loop(0, chips, backward, 0)
    for core in (1 - c, c):
        v = m.act[pl.ds(core * 2 * rows, 2 * rows)].reshape(rows * 32, hidden)
        m.big[1, core] = dot_nt(v, m.we[...]).reshape(m.big.shape[2:])
        if core is not c:
            sg_copy = send_to(m.big.at[1, 1 - c], m.sg_in, m.pair_sem, 3, b, sibling)
            sg_copy.start()
    send_to(m.big.at[0, c], m.b2_in, m.pair_sem, 2, b, sibling).wait_recv()
    send_to(m.big.at[1, c], m.sg_in, m.pair_sem, 3, b, sibling).wait_recv()

    def finish(r, _):
        for p in range(2):
            rp = 2 * r + p
            grad = m.big[1, c, rp] + m.sg_in[rp]
            v = m.res[rp]
            n, inv = ln_parts(v)
            branch = m.b1[(rows // 2) * lax.rem(rp, 4) + rp // 4]
            up = m.ctd[rp].astype(F32)
            m.acc[1] += grad
            m.acc[2] += grad * n
            back = up + ln_back(grad * scale2, n, inv)
            m.rg[rp] = back
            m.acc[3] += back * branch
            one = (back * gate1).astype(BF16)
            m.og[lax.rem(rp, 4), rp // 4] = one
            m.acc[4] += one.astype(F32)
            branch2 = m.big[0, c, rp] + m.b2_in[rp] + rb
            m.acc[5] += up * branch2
            interleave(m.rowf, r, p, v + gate2 * branch2)
        m.out[r] = joined(m.rowf, r).astype(BF16)
        return 0

    lax.fori_loop(0, rows, finish, 0, unroll=2)
    out_copy = pltpu.make_async_copy(m.out, m.out_hbm, m.load_sem.at[13])
    out_copy.start()

    to_groups(m.og, m.gg, m.gg_sem, m.gg_sem2)

    pack = []
    for v in (m.acc[3], m.acc[1], m.acc[2], m.acc[5]):
        pair = halves(v)
        for h in range(2):
            pack += [pair[h : h + 1, 0:half], pair[h : h + 1, half:]]
    def own_sums(buffer, sems, value):
        buffer[b, c, z] = value.astype(BF16)
        for d in range(1, chips):
            start(send_to(buffer.at[b, c, z], buffer.at[b, c, z], sems, d, b, 2 * chip(d) + c))

    def to_canvases(buffer, sems, sems2):
        for d in range(1, chips):
            i = chip(chips - d)
            send_to(buffer.at[b, c, i], buffer.at[b, c, i], sems, d, b, 2 * i + c).wait_recv()
        for e in range(1, 4):
            start(send_to(buffer.at[b, c], buffer.at[b, c], sems2, e, lax.rem(b + e, 4), s))

    def to_sibling(buffer, sems2, sems3):
        for e in range(1, 4):
            i = lax.rem(b - e + 4, 4)
            send_to(buffer.at[i, c], buffer.at[i, c], sems2, e, i, s).wait_recv()
        start(send_to(buffer.at[:, c], buffer.at[:, c], sems3, 0, b, sibling))

    def from_sibling(buffer, sems3):
        send_to(buffer.at[:, c], buffer.at[:, 1 - c], sems3, 0, b, sibling).wait_recv()

    own_sums(m.late, m.late_sem, jnp.concatenate(pack, axis=0))
    sums_ob = jnp.sum(m.acc[4], axis=0, keepdims=True)
    sums_rb = jnp.sum(m.acc[0], axis=0, keepdims=True)
    pad_lanes = jnp.zeros((1, half - own), F32)
    pad_rows = jnp.zeros((4, half), F32)
    for t in range(strips):
        piece = jnp.concatenate(
            [
                jnp.where(c == t % 2, m.hkg[t // 2, 0:10], 0.0),
                jnp.concatenate([sums_ob[:, t * own : t * own + own], pad_lanes], axis=1),
                jnp.concatenate([sums_rb[:, t * own : t * own + own], pad_lanes], axis=1),
                pad_rows,
            ],
            axis=0,
        )
        m.piece[t] = piece.astype(BF16)
    for d in range(1, strips):
        t = lax.rem(s + d, strips)
        start(send_to(m.piece.at[t], m.piece_in.at[d], m.piece_sem, d, b, t))

    pass_on(m.gg, m.gg_sem, m.gg_sem2, 0)
    c_half(0)
    c_half(1)
    pass_on(m.gg, m.gg_sem, m.gg_sem2, 1)
    c_half(2)
    pass_on(m.gg, m.gg_sem, m.gg_sem2, 2)
    pass_on(m.gg, m.gg_sem, m.gg_sem2, 3)
    c_half(3)
    to_canvases(m.late, m.late_sem, m.late_sem2)
    for n in range(chips):
        r_quarter(n)
    r_spread()
    groups_ready(m.gg, m.gg_sem2)
    wo_own = m.wo[pl.ds(pl.multiple_of(c * half, 128), half), :]
    w = dot_nt(m.gg[...].reshape(total, width), wo_own).astype(BF16)
    for n in range(3):
        m.da[n] = w[:, n * 128 : n * 128 + 128]

    for n in range(3):
        other = (1 - c) * 3 + n
        send_to(m.ag.at[other], m.ag.at[other], m.ag_sem, n, b, sibling).wait_recv()
    columns = m.gg[:, :, :, pl.ds(pl.multiple_of(c * half, 128), half)].reshape(total, half)
    full = jnp.concatenate([m.ag[n] for n in range(6)], axis=-1)
    m.jo[3] = dot_tn(full, columns).astype(BF16).reshape(m.jo.shape[1:])
    c_begin(7)

    tops = lax.broadcasted_iota(jnp.int32, (128, total), 0) < 64
    group = m.mg[...].reshape(total, width)
    for n in range(3):
        d2 = m.da[n]
        outs = []
        for h in range(2):
            dp = dot_nt(head(d2, h), m.qkv[6 + n])
            probs = m.probs[n, h].astype(F32)
            inner = jnp.sum(probs * dp, axis=-1, keepdims=True)
            m.ds[h] = (probs * (dp - inner)).astype(BF16)
            outs.append(dot(m.ds[h], m.qkv[3 + n]))
        dq = (jnp.where(lane, outs[0], outs[1]) * factor).astype(BF16)
        dk = [dot_tn(m.qkv[n], m.ds[h]) for h in range(2)]
        dk = (jnp.where(tops, dk[0], dk[1]) * factor).T.astype(BF16)
        dv = [dot_tn(d2, m.probs[n, h]) for h in range(2)]
        dv = jnp.where(tops, dv[0], dv[1]).T.astype(BF16)
        m.dqkv[n] = dq
        m.dqkv[3 + n] = dk
        m.dqkv[6 + n] = dv
        w = dot_tn(group, jnp.concatenate([dq, dk, dv], axis=-1))
        m.jo[n] = w.astype(BF16).reshape(m.jo.shape[1:])
        c_begin(4 + n)

    r_across()
    for j in range(4):
        c_quarter(j)

    b2_copy.wait_send()
    sg_copy.wait_send()

    def partial(core):
        strip_rows = [
            jnp.concatenate(
                [
                    m.dqkv[k, pl.ds(pl.multiple_of((2 * i + core) * 64, 64), 64), :]
                    for i in range(chips)
                ],
                axis=0,
            )
            for k in range(9)
        ]
        w = None
        for part in range(3):
            v = jnp.concatenate(strip_rows[3 * part : 3 * part + 3], axis=-1)
            v = dot_nt(v, m.wj[part])
            w = v if w is None else w + v
        m.big[0, core] = w.reshape(m.big.shape[2:])

    partial(1 - c)
    start(send_to(m.big.at[0, 1 - c], m.mp_in, m.pair_sem, 4, b, sibling))
    partial(c)
    send_to(m.big.at[0, c], m.mp_in, m.pair_sem, 4, b, sibling).wait_recv()
    four = rows // 2
    for d in range(chips):
        i = chip(d)
        at = pl.ds(four * i, four)
        low = (m.big[0, c, at] + m.mp_in[at]).astype(BF16)
        if d:
            m.mo[i] = low
            start(send_to(m.mo.at[i], m.mr.at[z], m.mr_sem, d, b, 2 * i + c))
        else:
            m.mr[z] = low

    to_sibling(m.late, m.late_sem2, m.late_sem3)
    sums = m.piece[s].astype(F32)
    for d in range(1, strips):
        send_to(m.piece.at[0], m.piece_in.at[d], m.piece_sem, d, b, s).wait_recv()
        sums = sums + m.piece_in[d].astype(F32)
    m.small[b] = sums.astype(BF16)
    for e in range(1, 4):
        start(send_to(m.small.at[b], m.small.at[b], m.small_sem, e, lax.rem(b + e, 4), s))
    c_spread(0)
    c_spread(1)
    c_half(7)
    c_half(4)
    c_half(5)
    c_half(6)

    for d in range(1, chips):
        i = chip(chips - d)
        send_to(m.mo.at[i], m.mr.at[i], m.mr_sem, d, b, 2 * i + c).wait_recv()
    for r in (0, rows - 1):
        for p in range(2):
            m.md[r + 1, p] = m.mr[(r % 2) * 2 + p, r // 2]
    start_edges(m.md, m.md_sem)
    c_spread(2)
    c_spread(3)
    c_across(0)
    c_across(1)
    r_sum()
    for r in range(1, rows - 1):
        for p in range(2):
            m.md[r + 1, p] = m.mr[(r % 2) * 2 + p, r // 2]

    m.acc1[...] = jnp.zeros_like(m.acc1)

    def mixer_rows(low, high):
        for k in range(width // 128):
            lanes = pl.ds(k * 128, 128)
            weights = [m.mk[t : t + 1, k * 128 : k * 128 + 128] for t in range(9)]

            def line(r, p):
                return m.md[r, p, :, lanes]

            def step(r, carry):
                new = window(line, r + 2)
                three = (carry[0], carry[1], new)
                out = conv(three, weights, True)
                for p in range(2):
                    m.fg[2 * r + p, :, lanes] = out[p]
                centre = [m.fp[r + 1, p, :, lanes].astype(F32) for p in range(2)]
                return carry[1], new, tuple(taps(three, centre, carry[2]))

            begin = tuple(m.acc1[t, :, lanes] for t in range(9))
            _, _, sums = lax.fori_loop(
                low, high, step, (window(line, low), window(line, low + 1), begin), unroll=True
            )
            for t in range(9):
                m.acc1[t, :, lanes] = sums[t]

    m.acc[1] = jnp.zeros_like(m.acc[1])
    m.acc[2] = jnp.zeros_like(m.acc[2])

    def token_row(r, _):
        for p in range(2):
            rp = 2 * r + p
            grad = m.fg[rp]
            n, inv = ln_parts(m.xd[r, p].astype(F32))
            m.acc[1] += grad
            m.acc[2] += grad * n
            interleave(m.rowf, r, p, m.rg[rp] + ln_back(grad * scale1, n, inv))
        m.tgo[r] = joined(m.rowf, r)
        return 0

    mixer_rows(1, rows - 1)
    lax.fori_loop(1, rows - 1, token_row, 0, unroll=3)
    top_edge(m.md, m.md_sem)
    mixer_rows(0, 1)
    token_row(0, 0)
    bottom_edge(m.md, m.md_sem)
    mixer_rows(rows - 1, rows)
    token_row(rows - 1, 0)
    tg_copy = pltpu.make_async_copy(m.tgo, m.tg_hbm, m.load_sem.at[14])
    tg_copy.start()

    pack = []
    third = width // 3
    for v in (m.acc[1], m.acc[2]):
        pair = halves(v)
        for h in range(2):
            pack += [pair[h : h + 1, k * third : k * third + third] for k in range(3)]
    pack.append(jnp.zeros((4, third), F32))
    own_sums(m.early, m.early_sem, jnp.concatenate(pack, axis=0))
    mixer_sums = [jnp.sum(m.acc1[t], axis=0, keepdims=True) for t in range(9)]
    mixer_sums = jnp.concatenate(mixer_sums + [jnp.zeros((7, width), F32)], axis=0)
    pad_lanes = jnp.zeros((16, 128 - own), F32)
    for t in range(strips):
        m.mpiece[t] = jnp.concatenate(
            [mixer_sums[:, t * own : t * own + own], pad_lanes], axis=1
        ).astype(BF16)
    for d in range(1, strips):
        t = lax.rem(s + d, strips)
        start(send_to(m.mpiece.at[t], m.mpiece_in.at[d], m.mpiece_sem, d, b, t))

    for j in (7, 4, 5, 6):
        c_quarter(j)
        c_spread(j)
    c_across(2)
    c_across(3)
    c_sum(0)
    c_sum(1)
    to_canvases(m.early, m.early_sem, m.early_sem2)
    c_across(7)
    c_sum(2)
    c_sum(3)
    c_across(4)
    sums = m.mpiece[s].astype(F32)
    for d in range(1, strips):
        send_to(m.mpiece.at[0], m.mpiece_in.at[d], m.mpiece_sem, d, b, s).wait_recv()
        sums = sums + m.mpiece_in[d].astype(F32)
    m.msmall[b] = sums.astype(BF16)
    for e in range(1, 4):
        start(send_to(m.msmall.at[b], m.msmall.at[b], m.msmall_sem, e, lax.rem(b + e, 4), s))
    c_across(5)
    c_sum(7)
    to_sibling(m.early, m.early_sem2, m.early_sem3)
    c_across(6)
    for j in (4, 5, 6):
        c_sum(j)

    finals = []

    def store(src, dst, index):
        cp = pltpu.make_async_copy(src, dst, m.load_sem.at[index])
        cp.start()
        finals.append(cp)

    for e in range(1, 4):
        i = lax.rem(b - e + 4, 4)
        send_to(m.cond_all.at[i], m.cond_all.at[i], m.cond_sem, e, i, s).wait_recv()
        send_to(m.small.at[i], m.small.at[i], m.small_sem, e, i, s).wait_recv()
        send_to(m.msmall.at[i], m.msmall.at[i], m.msmall_sem, e, i, s).wait_recv()
        send_to(m.r_all.at[i], m.r_all.at[i], m.r4_sem, e, i, s).wait_recv()
    store(m.r_all, m.r_hbm, 15)
    store(m.cond_all, m.cond_hbm, 16)
    store(m.small, m.small_hbm, 17)
    store(m.msmall, m.msmall_hbm, 18)
    from_sibling(m.late, m.late_sem3)
    from_sibling(m.early, m.early_sem3)
    store(m.late, m.late_hbm, 19)
    store(m.early, m.early_hbm, 20)
    for j in range(8):
        for xs in range(2):
            for cs in range(2):
                source = 2 * c + xs
                e = lax.rem(b - source + 4, 4)
                local = jnp.logical_and(source == b, cs == c)

                @pl.when(jnp.logical_not(local))
                def _():
                    pltpu.make_async_remote_copy(
                        src_ref=m.c_out.at[j],
                        dst_ref=m.c_all.at[j, xs, cs],
                        send_sem=m.c4_sem[0].at[j, e],
                        recv_sem=m.c4_sem[1].at[j, e, cs],
                        device_id=(source, 2 * z + cs),
                        device_id_type=MESH,
                    ).wait_recv()

    store(m.c_all, m.c_hbm, 21)
    for cp in sent:
        cp.wait_send()
    edges_sent(m.fp, m.fp_sem)
    edges_sent(m.md, m.md_sem)

    halo_sent(m.ex, m.ex_sem)
    halo_sent(m.cg, m.cg_sem)
    for h in range(2):
        for n in range(chips):
            r_one(n, h).wait_send()
            r_two(n, h).wait_send()
        for j in range(8):
            c_one(j, h).wait_send()
            c_two(j, h).wait_send()
    for k in range(3):
        r_three(k).wait_send()
        r_four(k + 1).wait_send()
        for j in range(8):
            c_three(j, k).wait_send()
            c_four(j, k + 1).wait_send()

    @pl.when(c != y)
    def _():
        for j in range(8):
            c_four(j, 0).wait_send()

    out_copy.wait()
    tg_copy.wait()
    for cp in finals:
        cp.wait()


def block(tokens, mod, mixer, owner, cond, ob, eb, hk, rb, wj, wo, we, wr, cot, strips):
    rows, cols, width = tokens.shape
    chips = strips // 2
    half = width // 2
    total = strips * 64
    blocks = 2 * rows
    chip_rows = 2 * rows
    part = width // chips // 4
    third = width // 3
    shape = jax.ShapeDtypeStruct
    vm = pltpu.VMEM

    def dma(*size):
        return pltpu.SemaphoreType.DMA(size)

    ins = dict(
        tok=tokens, mod=mod, mixer=mixer, owner=owner, cond=cond, ob=ob, eb=eb, hidden=hk, rb=rb,
        wj_hbm=wj, wo_hbm=wo, we_hbm=we, wr_hbm=wr, cot_hbm=cot,
    )
    outs = dict(
        out_hbm=shape((rows, cols, width), BF16),
        tg_hbm=shape((rows, cols, width), F32),
        r_hbm=shape((4, 2, width // 8, half), BF16),
        c_hbm=shape((8, 2, 2, part, half), BF16),
        cond_hbm=shape((4,) + cond.shape, F32),
        small_hbm=shape((4, 16, half), BF16),
        msmall_hbm=shape((4, 16, 128), BF16),
        late_hbm=shape((4, 2, chips, 16, half), BF16),
        early_hbm=shape((4, 2, chips, 16, third), BF16),
    )
    scratch = dict(
        mk=vm((9, width), F32),
        ebf=vm((1, 2 * chips * half), F32),
        hk=vm((chips, 9, half), F32),
        wj=vm((3, width, half), BF16),
        wo=vm((width, width), BF16),
        we=vm((width, chips * half), BF16),
        wr=vm((chips * half, width), BF16),
        cot=vm((rows, cols, width), BF16),
        cond_all=vm((4,) + cond.shape, F32),
        rowf=vm((rows, width // 128, cols, 128), F32),
        xd=vm((rows, 2, 16, width), BF16),
        fp=vm((rows + 2, 2, 16, width), BF16),
        ms=vm((chips, rows // 2, 16, width), BF16),
        mg=vm((strips, rows // 2, 16, width), BF16),
        qkv=vm((9, total, 128), BF16),
        probs=vm((3, 2, total, total), BF16),
        ag=vm((6, total, 128), BF16),
        ai=vm((6, chips, 64, 128), BF16),
        acc=vm((6, 16, width), F32),
        acc1=vm((9, 8, width), F32),
        ctd=vm((blocks, 16, width), BF16),
        tg=vm((2, blocks, 16, width), BF16),
        sc=vm((2, blocks, 16, width), BF16),
        b1=vm((blocks, 16, width), F32),
        res=vm((blocks, 16, width), F32),
        ex=vm((chip_rows + 2, 2, 16, chips * half), BF16),
        cg=vm((chip_rows + 2, 2, 16, chips * half), BF16),
        act=vm((2 * blocks, 16, chips * half), BF16),
        big=vm((2, 2, blocks, 16, width), F32),
        b2_in=vm((blocks, 16, width), F32),
        sg_in=vm((blocks, 16, width), F32),
        hkg=vm((chips, 16, half), F32),
        rg=vm((blocks, 16, width), F32),
        og=vm((chips, rows // 2, 16, width), BF16),
        out=vm((rows, cols, width), BF16),
        gg=vm((strips, rows // 2, 16, width), BF16),
        da=vm((3, total, 128), BF16),
        ds=vm((2, total, total), BF16),
        dqkv=vm((9, total, 128), BF16),
        mp_in=vm((blocks, 16, width), F32),
        mo=vm((chips, rows // 2, 16, width), BF16),
        mr=vm((chips, rows // 2, 16, width), BF16),
        md=vm((rows + 2, 2, 16, width), BF16),
        fg=vm((blocks, 16, width), F32),
        tgo=vm((rows, cols, width), F32),
        rw=vm((chips, 2, 2, width // 4, half), BF16),
        r1=vm((chips, 2, 2, width // 8, half), BF16),
        r2=vm((chips, 2, width // 8, half), BF16),
        r3=vm((3, 2, width // 8, half), BF16),
        r_all=vm((4, 2, width // 8, half), BF16),
        ew=vm((4, chips, 2, 2, part, half), BF16),
        jo=vm((4, chips, 2, 2, part, half), BF16),
        c1=vm((8, 2, 2, 2, part, half), BF16),
        c2=vm((8, chips, part, half), BF16),
        c3=vm((8, 3, part, half), BF16),
        c_out=vm((8, part, half), BF16),
        c_all=vm((8, 2, 2, part, half), BF16),
        late=vm((4, 2, chips, 16, half), BF16),
        early=vm((4, 2, chips, 16, third), BF16),
        piece=vm((strips, 16, half), BF16),
        piece_in=vm((strips, 16, half), BF16),
        small=vm((4, 16, half), BF16),
        mpiece=vm((strips, 16, 128), BF16),
        mpiece_in=vm((strips, 16, 128), BF16),
        msmall=vm((4, 16, 128), BF16),
        load_sem=dma(22),
    )
    pairs = dict(
        cond_sem=(4,), fp_sem=(2,), md_sem=(2,), mg_sem=(chips,), mg_sem2=(chips,),
        gg_sem=(chips,), gg_sem2=(chips,), ai_sem=(3, strips), ag_sem=(3,), pair_sem=(5,),
        ex_sem=(2,), cg_sem=(2,), mr_sem=(chips,),
        r1_sem=(chips, 2), r2_sem=(chips, 2), r3_sem=(3,), r4_sem=(4,),
        c1_sem=(8, 2), c2_sem=(8, 2), c3_sem=(8, 3),
        late_sem=(chips,), late_sem2=(4,), late_sem3=(1,),
        early_sem=(chips,), early_sem2=(4,), early_sem3=(1,),
        piece_sem=(strips,), small_sem=(4,), mpiece_sem=(strips,), msmall_sem=(4,),
    )
    names = list(ins) + list(outs) + list(scratch)
    shapes = list(scratch.values())
    for size in list(pairs.values()):
        shapes += [dma(*size), dma(*size)]
    shapes += [dma(8, 4), dma(8, 4, 2)]
    plain = len(names)

    def kernel(*refs):
        named = list(refs[:plain])
        sems = refs[plain:]
        both = [(sems[2 * i], sems[2 * i + 1]) for i in range(len(sems) // 2)]
        block_kernel(names + list(pairs) + ["c4_sem"], *named, *both)

    return pl.pallas_call(
        kernel,
        name="block",
        out_shape=tuple(outs.values()),
        in_specs=[WHOLE] * 3 + [SCALARS] + [WHOLE] * 5 + [LEFT] * 5,
        out_specs=(LEFT,) * len(outs),
        scratch_shapes=shapes,
        compiler_params=pltpu.CompilerParams(
            collective_id=0, has_side_effects=True, vmem_limit_bytes=VMEM_BYTES
        ),
    )(*ins.values())


def final_kernel(
    out_in, tg_in, r_in, c_in, cond_ref, small_ref, msmall_ref, late_ref, early_ref, aw_hbm,
    out_ref, tg_ref, tab_ref, ad_out, ab_ref, mix_ref, joint_out, output_out, ob_ref,
    expand_out, eb_ref, hidden_ref, reduce_out, rb_ref,
    aw, out_v, tg_v, r_ref, c_ref, ad_ref, joint_ref, output_ref, expand_ref, reduce_ref, sem,
):
    s = lax.axis_index("strip")
    strips = lax.axis_size("strip")
    width = cond_ref.shape[2] - 256
    own = width // strips
    half = width // 2
    third = width // 3
    loads = [
        (r_in, r_ref),
        (c_in, c_ref),
        (aw_hbm.at[pl.ds(pl.multiple_of(s * own, 16), own)], aw),
        (out_in, out_v),
        (tg_in, tg_v),
    ]
    loads = [pltpu.make_async_copy(a, v, sem.at[i]) for i, (a, v) in enumerate(loads)]
    for cp in loads:
        cp.start()
    stores = []

    def store(src, dst):
        cp = pltpu.make_async_copy(src, dst, sem.at[5 + len(stores)])
        cp.start()
        stores.append(cp)

    small = small_ref[0].astype(F32)
    mixer = msmall_ref[0].astype(F32)
    for i in range(1, 4):
        small = small + small_ref[i].astype(F32)
        mixer = mixer + msmall_ref[i].astype(F32)
    hidden_ref[...] = small[0:9]
    eb_ref[...] = small[9]
    ob_ref[...] = small[10, 0:own]
    rb_ref[...] = small[11, 0:own]
    mix_ref[...] = mixer[0:9, 0:own]

    n = width // 4
    loads[0].wait()
    for q in range(4):
        reduce_ref[:, q * n : q * n + n] = r_ref[q].reshape(n, half).astype(F32).T
    store(reduce_ref, reduce_out)
    loads[1].wait()
    part = c_ref.shape[3]
    for xs in range(2):
        rows = slice(xs * part, xs * part + part)
        for cs in range(2):
            for k in range(4):
                at = (2 * k + cs) * half
                expand_ref[rows, at : at + half] = c_ref[k, xs, cs].astype(F32)
            for k in range(3):
                for p in range(3):
                    at = p * width + cs * half + k * 128
                    joint_ref[rows, at : at + 128] = c_ref[
                        4 + k, xs, cs, :, p * 128 : p * 128 + 128
                    ].astype(F32)
            output_ref[rows, cs * half : cs * half + half] = c_ref[7, xs, cs].astype(F32)
    store(expand_ref, expand_out)
    store(joint_ref, joint_out)
    store(output_ref, output_out)
    loads[3].wait()
    store(out_v, out_ref)
    loads[4].wait()
    store(tg_v, tg_ref)

    slots = 32
    condition = cond_ref[...].reshape(slots, width + 256)
    labels = condition[:, width : width + 1]
    slot_late = jnp.concatenate([cond_ref[i, 0:1, width + 128 :] for i in range(4)], axis=1)
    slot_early = jnp.concatenate([cond_ref[i, 1:2, width + 128 :] for i in range(4)], axis=1)
    condition = condition[:, 0:width]
    pick = lax.broadcasted_iota(jnp.int32, (width, own), 0) == (
        lax.broadcasted_iota(jnp.int32, (width, own), 1) + s * own
    )
    pick = jnp.where(pick, 1.0, 0.0)
    condition = jnp.dot(
        condition, pick, precision=lax.Precision.HIGHEST, preferred_element_type=F32
    )
    sigmoid = 1.0 / (1.0 + jnp.exp(-condition))
    silu = (condition * sigmoid).astype(BF16)
    slope = sigmoid * (1.0 + condition * (1.0 - sigmoid))

    count = 4 * strips * 16
    row = lax.rem(lax.broadcasted_iota(jnp.int32, (slots, count), 1), 16)
    index = lax.broadcasted_iota(jnp.int32, (slots, count), 0)
    hit_late = index == slot_late.astype(jnp.int32)
    hit_early = index == slot_early.astype(jnp.int32)
    late = late_ref[...].reshape(count, half)
    early = early_ref[...].reshape(count, third)
    loads[2].wait()
    bias = jnp.zeros((1, 6 * own), F32)
    sums = []
    silu_grad = jnp.zeros((slots, own), F32)
    pieces = []
    for i in range(2):
        for k in range(3):
            mine = jnp.logical_or(row == 6 * i + k, row == 6 * i + 3 + k)
            pieces.append((early, jnp.logical_and(hit_early, mine), i * width + k * third, third))
    for i in range(4):
        for k in range(2):
            mine = jnp.logical_or(row == 4 * i + k, row == 4 * i + 2 + k)
            pieces.append((late, jnp.logical_and(hit_late, mine), (2 + i) * width + k * half, half))
    for source, mine, at, size in pieces:
        chosen = jnp.where(mine, 1.0, 0.0).astype(BF16)
        grad = dot(chosen, source)
        sums.append(jnp.sum(grad, axis=0, keepdims=True))
        low = grad.astype(BF16)
        ad_ref[:, at : at + size] = dot_tn(silu, low)
        silu_grad = silu_grad + dot_nt(low, aw[:, at : at + size])
    store(ad_ref, ad_out)
    sums = jnp.concatenate(sums, axis=1)
    for t in range(strips):
        bias = jnp.where(s == t, sums[:, t * 6 * own : t * 6 * own + 6 * own], bias)
    ab_ref[...] = bias[0]
    classes = tab_ref.shape[1]
    onehot = lax.broadcasted_iota(jnp.int32, (slots, classes), 1) == labels.astype(jnp.int32)
    tab_ref[...] = lax.dot_general(
        silu_grad * slope,
        jnp.where(onehot, 1.0, 0.0),
        TN,
        precision=lax.Precision.HIGHEST,
        preferred_element_type=F32,
    )
    for cp in stores:
        cp.wait()


def final(parts, aw, classes, strips):
    out, tg, r, c = parts[:4]
    width = out.shape[-1]
    own = width // strips
    half = width // 2
    shape = jax.ShapeDtypeStruct
    vm = pltpu.VMEM
    return pl.pallas_call(
        final_kernel,
        name="final",
        out_shape=(
            shape(out.shape, BF16),
            shape(tg.shape, F32),
            shape((own, classes), F32),
            shape((own, 6 * width), F32),
            shape((6 * own,), F32),
            shape((9, own), F32),
            shape((own, 3 * width), F32),
            shape((own, width), F32),
            shape((own,), F32),
            shape((own, 4 * width), F32),
            shape((half,), F32),
            shape((9, half), F32),
            shape((half, width), F32),
            shape((own,), F32),
        ),
        in_specs=[LEFT] * 4 + [WHOLE] * 5 + [LEFT],
        out_specs=(
            LEFT, LEFT, WHOLE, LEFT, WHOLE, WHOLE, LEFT, LEFT, WHOLE, LEFT, WHOLE, WHOLE, LEFT,
            WHOLE,
        ),
        scratch_shapes=[
            vm((own, 6 * width), BF16),
            vm(out.shape, BF16),
            vm(tg.shape, F32),
            vm(r.shape, BF16),
            vm(c.shape, BF16),
            vm((own, 6 * width), F32),
            vm((own, 3 * width), F32),
            vm((own, width), F32),
            vm((own, 4 * width), F32),
            vm((half, width), F32),
            pltpu.SemaphoreType.DMA((12,)),
        ],
        compiler_params=pltpu.CompilerParams(vmem_limit_bytes=VMEM_BYTES),
    )(*parts, aw)


def local_grouped(
    tokens, tile_owner, time_steps, class_labels, class_embedding_matrix, adaptive_weight,
    adaptive_bias, mixer_kernel, joint_weight, output_weight, output_bias, expand_weight,
    expand_bias, hidden_kernel, reduce_weight, reduce_bias, output_cotangent,
):
    strips = lax.axis_size("strip")
    owner = tile_owner.transpose(0, 2, 1)
    mod, cond = conditioning(
        owner, time_steps, class_labels, class_embedding_matrix.T, adaptive_bias,
        adaptive_weight,
    )
    parts = block(
        tokens[0], mod, mixer_kernel.T, owner, cond, output_bias, expand_bias,
        hidden_kernel.T, reduce_bias, joint_weight, output_weight, expand_weight, reduce_weight,
        output_cotangent[0], strips,
    )
    classes = class_embedding_matrix.shape[1]
    (
        out, tg, table, adaptive, bias, mixer, joint, output, ob, expand, eb, hidden, reduce, rb,
    ) = final(parts, adaptive_weight, classes, strips)
    return (
        out[None], tg[None], table, adaptive, bias, mixer.T, joint, output, ob, expand, eb,
        hidden.T, reduce, rb,
    )


EXACT_PRECISION = lax.Precision.HIGHEST


def padded_2(block, sides, width):
    for axis, dim in sides:
        count = lax.axis_size(axis)
        forward = [(i, i + 1) for i in range(count - 1)]
        backward = [(target, source) for source, target in forward]
        low = lax.ppermute(
            lax.slice_in_dim(block, block.shape[dim] - width, None, axis=dim), axis, forward
        )
        high = lax.ppermute(lax.slice_in_dim(block, 0, width, axis=dim), axis, backward)
        block = jnp.concatenate([low, block, high], axis=dim)
    return block


def normalize(values):
    centre = jnp.mean(values, axis=-1, keepdims=True)
    centred = values - centre
    spread = jnp.mean(centred * centred, axis=-1, keepdims=True)
    return centred * lax.rsqrt(spread + EPSILON)


def modulate(values, shifting, scaling):
    return normalize(values) * (1.0 + scaling) + shifting


def depthwise(padded, kernel):
    row_count = padded.shape[-3] - 2
    column_total = padded.shape[-2]
    widened = jnp.pad(padded, [(0, 0)] * (padded.ndim - 2) + [(1, 1), (0, 0)])
    result = jnp.zeros(
        padded.shape[:-3] + (row_count, column_total, padded.shape[-1]), padded.dtype
    )
    for tapping in range(9):
        row_shift = tapping // 3
        col_shift = tapping % 3
        window = lax.slice_in_dim(widened, row_shift, row_shift + row_count, axis=widened.ndim - 3)
        window = lax.slice_in_dim(
            window, col_shift, col_shift + column_total, axis=widened.ndim - 2
        )
        result = result + kernel[:, tapping] * window
    return result


def kernel_grad(padded, gradient):
    row_count = gradient.shape[1]
    column_total = gradient.shape[2]
    widened = jnp.pad(padded, ((0, 0), (0, 0), (1, 1), (0, 0)))
    columns = []
    for tapping in range(9):
        row_shift = tapping // 3
        col_shift = tapping % 3
        window = widened[
            :, row_shift : row_shift + row_count, col_shift : col_shift + column_total, :
        ]
        columns.append(jnp.sum(window * gradient, axis=(0, 1, 2)))
    return jnp.stack(columns, axis=1)


def timestep_features(time_steps, model_width):
    half_width = model_width // 2
    frequencies = jnp.exp(
        -math.log(10000.0) * jnp.arange(half_width, dtype=jnp.float32) / half_width
    )
    angles = time_steps.astype(jnp.float32)[..., None] * frequencies
    return jnp.concatenate([jnp.cos(angles), jnp.sin(angles)], axis=-1)


def group_owner(owner):
    canvases, row_count, column_total = owner.shape
    shaped = owner.reshape(canvases, row_count // 2, 2, column_total // 2, 2).transpose(
        0, 2, 4, 1, 3
    )
    return shaped.reshape(canvases, 2, 2, row_count // 2 * (column_total // 2))


def to_groups(tensor, head_count):
    canvases, row_count, column_total, features = tensor.shape
    head_size = features // head_count
    shaped = tensor.reshape(
        canvases, row_count // 2, 2, column_total // 2, 2, head_count, head_size
    )
    shaped = shaped.transpose(0, 2, 4, 5, 1, 3, 6)
    return shaped.reshape(
        canvases, 2, 2, head_count, row_count // 2 * (column_total // 2), head_size
    )


def from_groups(tensor, row_count, column_total):
    canvases, head_count, head_size = (tensor.shape[0], tensor.shape[3], tensor.shape[-1])
    shaped = tensor.reshape(
        canvases, 2, 2, head_count, row_count // 2, column_total // 2, head_size
    )
    shaped = shaped.transpose(0, 4, 1, 5, 2, 3, 6)
    return shaped.reshape(canvases, row_count, column_total, head_count * head_size)


def local(
    tokens,
    tile_owner,
    time_steps,
    class_labels,
    class_embedding_matrix,
    adaptive_weight,
    adaptive_bias,
    mixer_kernel,
    joint_weight,
    output_weight,
    output_bias,
    expand_weight,
    expand_bias,
    hidden_kernel,
    reduce_weight,
    reduce_bias,
    output_cotangent,
):
    canvases, row_count, column_total, model_width = tokens.shape
    head_count = HEADS
    head_size = model_width // head_count
    factor = head_size ** (-0.5)
    half_cols = column_total // 2
    strips = lax.axis_size("strip")
    strip_index = lax.axis_index("strip")
    canvas_rows = row_count * strips
    class_count = class_embedding_matrix.shape[1]
    latent_count = time_steps.shape[1]
    tile_rows = canvas_rows // 4
    full_owner = jnp.broadcast_to(
        tile_owner[:, :, None, :, None], (canvases, 4, tile_rows, 2, half_cols)
    ).reshape(canvases, canvas_rows, column_total)
    local_owner = lax.dynamic_slice_in_dim(full_owner, strip_index * row_count, row_count, 1)
    token_hot = (local_owner[..., None] == jnp.arange(latent_count, dtype=jnp.int32)).astype(
        jnp.float32
    )
    class_onehot = (class_labels[..., None] == jnp.arange(class_count, dtype=jnp.int32)).astype(
        jnp.bfloat16
    )
    class_rows = jnp.einsum(
        "ywj,gj->ywg", class_onehot, class_embedding_matrix, preferred_element_type=jnp.float32
    )
    condition = timestep_features(time_steps, model_width) + class_rows
    silu_value, silu_pull = jax.vjp(jax.nn.silu, condition)
    silu_cond = silu_value.astype(jnp.bfloat16)
    modulation = jnp.einsum(
        "cbd,de->cbe", silu_cond, adaptive_weight, preferred_element_type=jnp.float32
    )
    modulation = modulation + adaptive_bias.astype(jnp.float32)
    token_mod = jnp.einsum("crkb,cbe->crke", token_hot, modulation, precision=EXACT_PRECISION)
    shift_one, scale_one, gate_one, shift_two, scale_two, gate_two = jnp.split(
        token_mod, 6, axis=-1
    )
    inputs = tokens.astype(jnp.float32)
    first_value, first_pull = jax.vjp(modulate, inputs, shift_one, scale_one)
    first = first_value.astype(jnp.bfloat16)
    first_padded = padded_2(first, (("strip", 1),), 1)
    mixer_single_float = mixer_kernel.astype(jnp.float32)
    mixed = depthwise(first_padded.astype(jnp.float32), mixer_single_float).astype(jnp.bfloat16)
    joint = jnp.einsum("crkd,de->crke", mixed, joint_weight, preferred_element_type=jnp.float32)
    query_rows = joint[..., :model_width].astype(jnp.bfloat16)
    keys_local = joint[..., model_width : 2 * model_width].astype(jnp.bfloat16)
    values_local = joint[..., 2 * model_width :].astype(jnp.bfloat16)
    keys_canvas, values_canvas = (
        lax.all_gather(keys_local, "strip", axis=1, tiled=True),
        lax.all_gather(values_local, "strip", axis=1, tiled=True),
    )
    query_groups = to_groups(query_rows, head_count)
    key_groups = to_groups(keys_canvas, head_count)
    value_groups = to_groups(values_canvas, head_count)
    query_owner = group_owner(local_owner)
    key_owner = group_owner(full_owner)
    allowed = (query_owner[..., :, None] == key_owner[..., None, :])[:, :, :, None]

    def attention_scores():
        raw = (
            jnp.einsum(
                "cabhnd,cabhmd->cabhnm",
                query_groups,
                key_groups,
                preferred_element_type=jnp.float32,
            )
            * factor
        )
        return jnp.where(allowed, raw, MASKED)

    scores = attention_scores()
    peak = jnp.max(scores, axis=-1, keepdims=True)
    lifted_float = jnp.exp(scores - peak)
    total = jnp.sum(lifted_float, axis=-1, keepdims=True)
    softened = (lifted_float / total).astype(jnp.bfloat16)
    log_total = peak + jnp.log(total)
    attended_groups = jnp.einsum(
        "cabhnm,cabhmd->cabhnd", softened, value_groups, preferred_element_type=jnp.float32
    )
    attended = from_groups(attended_groups, row_count, column_total).astype(jnp.bfloat16)
    branch_one = jnp.einsum(
        "crkd,de->crke", attended, output_weight, preferred_element_type=jnp.float32
    )
    branch_one = branch_one + output_bias.astype(jnp.float32)
    residual = inputs + gate_one * branch_one
    second_value, second_pull = jax.vjp(modulate, residual, shift_two, scale_two)
    second = second_value.astype(jnp.bfloat16)
    expanded = jnp.einsum(
        "crkd,df->crkf", second, expand_weight, preferred_element_type=jnp.float32
    )
    expanded = (expanded + expand_bias.astype(jnp.float32)).astype(jnp.bfloat16)
    expanded_padded = padded_2(expanded, (("strip", 1),), 1)
    hidden_float = hidden_kernel.astype(jnp.float32)
    conv_out = depthwise(expanded_padded.astype(jnp.float32), hidden_float)
    gelu_value, gelu_pull = jax.vjp(jax.nn.gelu, conv_out)
    activated = gelu_value.astype(jnp.bfloat16)
    branch_two = jnp.einsum(
        "crkf,fd->crkd", activated, reduce_weight, preferred_element_type=jnp.float32
    )
    branch_two = branch_two + reduce_bias.astype(jnp.float32)
    outputs = (residual + gate_two * branch_two).astype(jnp.bfloat16)
    upstream = output_cotangent.astype(jnp.float32)
    two_grad = (upstream * gate_two).astype(jnp.bfloat16)
    gate_two_grad = upstream * branch_two
    reduce_bias_grad = jnp.sum(two_grad.astype(jnp.float32), axis=(0, 1, 2))
    reduce_weight_grad = jnp.einsum(
        "crkf,crkd->fd", activated, two_grad, preferred_element_type=jnp.float32
    )
    activated_grad = jnp.einsum(
        "crkd,fd->crkf", two_grad, reduce_weight, preferred_element_type=jnp.float32
    )
    conv_grad = gelu_pull(activated_grad)[0].astype(jnp.bfloat16)
    conv_padded = padded_2(conv_grad, (("strip", 1),), 1)
    expanded_grad = depthwise(conv_padded.astype(jnp.float32), hidden_float[:, ::-1]).astype(
        jnp.bfloat16
    )
    hidden_kernel_grad = kernel_grad(
        expanded_padded.astype(jnp.float32), conv_grad.astype(jnp.float32)
    )
    expand_bias_grad = jnp.sum(expanded_grad.astype(jnp.float32), axis=(0, 1, 2))
    expand_weight_grad = jnp.einsum(
        "crkd,crkf->df", second, expanded_grad, preferred_element_type=jnp.float32
    )
    second_grad = jnp.einsum(
        "crkf,df->crkd", expanded_grad, expand_weight, preferred_element_type=jnp.float32
    )
    residual_part, shift_two_grad, scale_two_grad = second_pull(second_grad)
    residual_grad = upstream + residual_part
    gate_one_grad = residual_grad * branch_one
    one_grad = (residual_grad * gate_one).astype(jnp.bfloat16)
    output_bias_grad = jnp.sum(one_grad.astype(jnp.float32), axis=(0, 1, 2))
    output_weight_grad = jnp.einsum(
        "crkd,crke->de", attended, one_grad, preferred_element_type=jnp.float32
    )
    attended_grad = jnp.einsum(
        "crke,de->crkd", one_grad, output_weight, preferred_element_type=jnp.float32
    ).astype(jnp.bfloat16)
    attended_grad_groups = to_groups(attended_grad, head_count)
    probs = jnp.exp(attention_scores() - log_total)
    prob_grads = jnp.einsum(
        "cabhnd,cabhmd->cabhnm",
        attended_grad_groups,
        value_groups,
        preferred_element_type=jnp.float32,
    )
    spread_sum = jnp.sum(probs * prob_grads, axis=-1, keepdims=True)
    score_grads = (probs * (prob_grads - spread_sum)).astype(jnp.bfloat16)
    query_grad_groups = (
        jnp.einsum(
            "cabhnm,cabhmd->cabhnd", score_grads, key_groups, preferred_element_type=jnp.float32
        )
        * factor
    )
    query_grad = from_groups(query_grad_groups, row_count, column_total).astype(jnp.bfloat16)
    all_queries, all_attended = (
        lax.all_gather(query_groups, "strip", axis=4, tiled=True),
        lax.all_gather(attended_grad_groups, "strip", axis=4, tiled=True),
    )
    all_logs, all_spreads = (
        lax.all_gather(log_total[..., 0], "strip", axis=4, tiled=True),
        lax.all_gather(spread_sum[..., 0], "strip", axis=4, tiled=True),
    )
    own_keys = to_groups(keys_local, head_count)
    own_values = to_groups(values_local, head_count)
    own_allowed = (key_owner[..., :, None] == query_owner[..., None, :])[:, :, :, None]
    own_scores = (
        jnp.einsum(
            "cabhnd,cabhmd->cabhnm", all_queries, own_keys, preferred_element_type=jnp.float32
        )
        * factor
    )
    own_scores = jnp.where(own_allowed, own_scores, MASKED)
    own_probs = jnp.exp(own_scores - all_logs[..., None])
    own_prob_grads = jnp.einsum(
        "cabhnd,cabhmd->cabhnm", all_attended, own_values, preferred_element_type=jnp.float32
    )
    own_score_grads = (own_probs * (own_prob_grads - all_spreads[..., None])).astype(jnp.bfloat16)
    key_grad_groups = (
        jnp.einsum(
            "cabhnm,cabhnd->cabhmd",
            own_score_grads,
            all_queries,
            preferred_element_type=jnp.float32,
        )
        * factor
    )
    value_grad_groups = jnp.einsum(
        "cabhnm,cabhnd->cabhmd",
        own_probs.astype(jnp.bfloat16),
        all_attended,
        preferred_element_type=jnp.float32,
    )
    key_grad = from_groups(key_grad_groups, row_count, column_total).astype(jnp.bfloat16)
    value_grad = from_groups(value_grad_groups, row_count, column_total).astype(jnp.bfloat16)
    joint_grad = jnp.concatenate([query_grad, key_grad, value_grad], axis=-1)
    joint_weight_grad = jnp.einsum(
        "crkd,crke->de", mixed, joint_grad, preferred_element_type=jnp.float32
    )
    mixed_grad = jnp.einsum(
        "crke,de->crkd", joint_grad, joint_weight, preferred_element_type=jnp.float32
    ).astype(jnp.bfloat16)
    mixed_padded = padded_2(mixed_grad, (("strip", 1),), 1)
    first_grad = depthwise(mixed_padded.astype(jnp.float32), mixer_single_float[:, ::-1])
    mixer_kernel_grad = kernel_grad(
        first_padded.astype(jnp.float32), mixed_grad.astype(jnp.float32)
    )
    input_part, shift_one_grad, scale_one_grad = first_pull(first_grad)
    tokens_grad = residual_grad + input_part
    token_grad = jnp.concatenate(
        [
            shift_one_grad,
            scale_one_grad,
            gate_one_grad,
            shift_two_grad,
            scale_two_grad,
            gate_two_grad,
        ],
        axis=-1,
    )
    modulation_grad = jnp.einsum("crkb,crke->cbe", token_hot, token_grad, precision=EXACT_PRECISION)
    silu_grad = jnp.einsum(
        "cbe,de->cbd",
        modulation_grad,
        adaptive_weight.astype(jnp.float32),
        precision=EXACT_PRECISION,
    )
    conditioning_grad = silu_pull(silu_grad)[0]
    table_grad = jnp.einsum(
        "soy,sok->yk",
        conditioning_grad,
        class_onehot.astype(jnp.float32),
        precision=EXACT_PRECISION,
    )
    adaptive_grad = jnp.einsum(
        "cbd,cbe->de", silu_cond.astype(jnp.float32), modulation_grad, precision=EXACT_PRECISION
    )
    adaptive_bias_grad = jnp.sum(modulation_grad, axis=(0, 1))
    (
        table_shard,
        adaptive_shard,
        adaptive_bias_shard,
        mixer_shard,
        joint_shard,
        output_shard,
        output_bias_shard,
        expand_shard,
        expand_bias_shard,
        hidden_shard,
        reduce_shard,
        reduce_bias_shard,
    ) = (
        lax.psum_scatter(
            table_grad.astype(jnp.bfloat16), "strip", scatter_dimension=0, tiled=True
        ).astype(jnp.float32),
        lax.psum_scatter(
            adaptive_grad.astype(jnp.bfloat16), "strip", scatter_dimension=0, tiled=True
        ).astype(jnp.float32),
        lax.psum_scatter(
            adaptive_bias_grad.astype(jnp.bfloat16), "strip", scatter_dimension=0, tiled=True
        ).astype(jnp.float32),
        lax.psum_scatter(
            mixer_kernel_grad.astype(jnp.bfloat16), "strip", scatter_dimension=0, tiled=True
        ).astype(jnp.float32),
        lax.psum_scatter(
            joint_weight_grad.astype(jnp.bfloat16), "strip", scatter_dimension=0, tiled=True
        ).astype(jnp.float32),
        lax.psum_scatter(
            output_weight_grad.astype(jnp.bfloat16), "strip", scatter_dimension=0, tiled=True
        ).astype(jnp.float32),
        lax.psum_scatter(
            output_bias_grad.astype(jnp.bfloat16), "strip", scatter_dimension=0, tiled=True
        ).astype(jnp.float32),
        lax.psum_scatter(
            expand_weight_grad.astype(jnp.bfloat16), "strip", scatter_dimension=0, tiled=True
        ).astype(jnp.float32),
        lax.psum_scatter(
            expand_bias_grad.astype(jnp.bfloat16), "strip", scatter_dimension=0, tiled=True
        ).astype(jnp.float32),
        lax.psum_scatter(
            hidden_kernel_grad.astype(jnp.bfloat16), "strip", scatter_dimension=0, tiled=True
        ).astype(jnp.float32),
        lax.psum_scatter(
            reduce_weight_grad.astype(jnp.bfloat16), "strip", scatter_dimension=0, tiled=True
        ).astype(jnp.float32),
        lax.psum_scatter(
            reduce_bias_grad.astype(jnp.bfloat16), "strip", scatter_dimension=0, tiled=True
        ).astype(jnp.float32),
    )
    summed = (
        lax.psum(table_shard.astype(jnp.bfloat16), "batch").astype(jnp.float32),
        lax.psum(adaptive_shard.astype(jnp.bfloat16), "batch").astype(jnp.float32),
        lax.psum(adaptive_bias_shard.astype(jnp.bfloat16), "batch").astype(jnp.float32),
        lax.psum(mixer_shard.astype(jnp.bfloat16), "batch").astype(jnp.float32),
        lax.psum(joint_shard.astype(jnp.bfloat16), "batch").astype(jnp.float32),
        lax.psum(output_shard.astype(jnp.bfloat16), "batch").astype(jnp.float32),
        lax.psum(output_bias_shard.astype(jnp.bfloat16), "batch").astype(jnp.float32),
        lax.psum(expand_shard.astype(jnp.bfloat16), "batch").astype(jnp.float32),
        lax.psum(expand_bias_shard.astype(jnp.bfloat16), "batch").astype(jnp.float32),
        lax.psum(hidden_shard.astype(jnp.bfloat16), "batch").astype(jnp.float32),
        lax.psum(reduce_shard.astype(jnp.bfloat16), "batch").astype(jnp.float32),
        lax.psum(reduce_bias_shard.astype(jnp.bfloat16), "batch").astype(jnp.float32),
    )
    return (
        outputs,
        tokens_grad,
        summed[0],
        summed[1],
        summed[2],
        summed[3],
        summed[4],
        summed[5],
        summed[6],
        summed[7],
        summed[8],
        summed[9],
        summed[10],
        summed[11],
    )


def solution(mesh):
    grouped = (mesh.shape["batch"], mesh.shape["strip"]) == (4, 8)
    return jax.shard_map(
        local_grouped if grouped else local,
        mesh=mesh,
        in_specs=(
            P("batch", "strip", None, None),
            P("batch", None, None),
            P("batch", None),
            P("batch", None),
            P(),
            P(),
            P(),
            P(),
            P(),
            P(),
            P(),
            P(),
            P(),
            P(),
            P(),
            P(),
            P("batch", "strip", None, None),
        ),
        out_specs=(
            P("batch", "strip", None, None),
            P("batch", "strip", None, None),
            P("strip", None),
            P("strip", None),
            P("strip"),
            P("strip", None),
            P("strip", None),
            P("strip", None),
            P("strip"),
            P("strip", None),
            P("strip"),
            P("strip", None),
            P("strip", None),
            P("strip"),
        ),
        check_vma=False,
    )
```

profile of v0, /device:TPU:0, one launch (start us, length us, event | category | flops | bytes accessed | tf_op | source)
XLA Modules:
  0.0 144.2 jit_solution(10769997078549148512)
XLA Ops:
  0.6 5.5 %conditioning.1 = (f32[2,4608]{1,0:T(2,128)}, f32[8,1024]{1,0:T(8,128)}) custom-call(s32[1,2,4]{2,1,0:T(2,128)} %bitcast.15, s32[1,8]{1,0:T(1,128)} %steps.1, s32[1,8]{1,0:T(1,128)} %labels.1, bf16[1000,768]{1,0:T(8,128)(2,1)} %bitcast.10, bf16[4608]{0:T(1024)(128)(2,1)} %ab.1, bf16[768,4608]{1,0:T(8,128)(2,1)} %aw_hbm.3), custom_call_target="tpu_custom_call" | custom-call | tf_op jit(solution)/shard_map/conditioning/pallas_call | solution.py:212
  6.2 129.6 %block.1 = (bf16[8,32,768]{2,1,0:T(8,128)(2,1)}, f32[8,32,768]{2,1,0:T(8,128)}, bf16[4,2,96,384]{3,2,1,0:T(8,128)(2,1)}, bf16[8,2,2,48,384]{4,3,2,1,0:T(8,128)(2...) custom-call(bf16[8,32,768]{2,1,0:T(8,128)(2,1)} %bitcast.11, ...), custom_call_target="tpu_custom_call" | custom-call | tf_op jit(solution)/shard_map/block/pallas_call | solution.py:1262
  135.8 8.3 %final.1 = (bf16[8,32,768]{2,1,0:T(8,128)(2,1)}, f32[8,32,768]{2,1,0:T(8,128)}, f32[96,1000]{1,0:T(8,128)}, f32[96,4608]{1,0:T(8,128)}, f32[576]{0:T(1024)}, /*i...) custom-call(bf16[8,32,768]{2,1,0:T(8,128)(2,1)} %get-tuple-element.4, ...), custom_call_target="tpu_custom_call" | custom-call | tf_op jit(solution)/shard_map/final/pallas_call | solution.py:1412
where the time goes:
time: 144 us
  Pallas kernels  143 us (99%)
    pallas_call x1, Pallas kernels, block(): pl.pallas_call(kernel, name='block', out_shape=tuple(outs.values()), in_s...  130 us
    pallas_call x1, Pallas kernels, final(): pl.pallas_call(final_kernel, name='final', out_shape=(shape(out.shape, BF...  8.3 us
    pallas_call x1, Pallas kernels, conditioning(): pl.pallas_call(condition_kernel, name='conditioning', out_shape=(shape((2...  5.52 us

commit v1 on v0

--- a/solution.py
+++ b/solution.py
@@ -45,7 +45,7 @@
     )
 
 
-def entry_barrier(strips):
+def entry_signals(strips):
     s = lax.axis_index("strip")
     b = lax.axis_index("batch")
     z = s // 2
@@ -62,7 +62,11 @@
                 barrier, inc=1, device_id=(lax.rem(b + e, 4), 2 * z + core), device_id_type=MESH
             )
             count += 1
-    pl.semaphore_wait(barrier, count)
+    return count
+
+
+def entry_wait(count):
+    pl.semaphore_wait(pltpu.get_barrier_semaphore(), count)
 
 
 def spread(mod, width):
@@ -151,73 +155,6 @@
     cdf = 0.5 + 0.5 * t
     slope = cdf + (0.5 * k0) * x * (1.0 - t * t) * (1.0 + (3.0 * 0.044715) * square)
     return x * cdf, slope
-
-
-def condition_kernel(owner, steps, labels, emb, ab, aw_hbm, mod_ref, cond_ref, aw, sem):
-    s = lax.axis_index("strip")
-    b = lax.axis_index("batch")
-    z = s // 2
-    classes, width = emb.shape
-    latents = steps.shape[1]
-    half = width // 2
-    copies = []
-    for i in range(6):
-        cp = pltpu.make_async_copy(aw_hbm.at[:, pl.ds(i * width, width)], aw.at[i], sem.at[i])
-        cp.start()
-        copies.append(cp)
-
-    row = lax.broadcasted_iota(jnp.int32, (latents, 1), 0)
-    when = jnp.zeros((latents, 1), F32)
-    label = jnp.zeros((latents, 1), jnp.int32)
-    for i in range(latents):
-        when = jnp.where(row == i, steps[0, i].astype(F32), when)
-        label = jnp.where(row == i, labels[0, i], label)
-    order = lax.broadcasted_iota(jnp.int32, (latents, half), 1).astype(F32)
-    angles = when * jnp.exp(-math.log(10000.0) * order / half)
-    features = jnp.concatenate([jnp.cos(angles), jnp.sin(angles)], axis=1)
-    onehot = lax.broadcasted_iota(jnp.int32, (latents, classes), 1) == label
-    condition = features + dot(jnp.where(onehot, 1.0, 0.0).astype(BF16), emb[...])
-    silu = (condition / (1.0 + jnp.exp(-condition))).astype(BF16)
-
-    lane = lax.broadcasted_iota(jnp.int32, (latents, 128), 1)
-    kind = lax.broadcasted_iota(jnp.int32, (latents, 128), 0)
-    line = lax.rem(lane, 16)
-    side = jnp.where(kind == 0, lax.rem(line // 2, 2), lax.rem(line // 3, 2))
-    tile = lax.rem(lane // 16, 4)
-    slots = jnp.zeros((latents, 128), jnp.int32)
-    for i in range(4):
-        for h in range(2):
-            hit = jnp.logical_and(tile == i, side == h)
-            slots = jnp.where(hit, owner[0, h, i] + b * latents, slots)
-    cond_ref[...] = jnp.concatenate(
-        [condition, jnp.broadcast_to(label.astype(F32), (latents, 128)), slots.astype(F32)], axis=1
-    )
-
-    bias = ab[...].astype(F32).reshape(1, 6 * width)
-    for i in range(6):
-        copies[i].wait()
-        lanes = slice(i * width, i * width + width)
-        table = dot(silu, aw[i]) + bias[:, lanes]
-        for h in range(2):
-            mine = row == owner[0, h, z]
-            mod_ref[h : h + 1, lanes] = jnp.sum(
-                jnp.where(mine, table, 0.0), axis=0, keepdims=True
-            )
-
-
-def conditioning(owner, steps, labels, emb, ab, aw):
-    width = emb.shape[1]
-    latents = steps.shape[1]
-    shape = jax.ShapeDtypeStruct
-    return pl.pallas_call(
-        condition_kernel,
-        name="conditioning",
-        out_shape=(shape((2, 6 * width), F32), shape((latents, width + 256), F32)),
-        in_specs=[SCALARS] * 3 + [WHOLE] * 2 + [LEFT],
-        out_specs=(WHOLE, WHOLE),
-        scratch_shapes=[pltpu.VMEM((6, width, width), BF16), pltpu.SemaphoreType.DMA((6,))],
-        compiler_params=pltpu.CompilerParams(vmem_limit_bytes=VMEM_BYTES),
-    )(owner, steps, labels, emb, ab, aw)
 
 
 def block_kernel(names, *refs):
@@ -252,6 +189,12 @@
         loads[name] = pltpu.make_async_copy(src, dst, m.load_sem.at[index])
         loads[name].start()
 
+    load("emb", m.emb_hbm, m.emb, 22)
+    for i in range(12):
+        lanes = pl.ds(i * half, half)
+        src = m.aw4_hbm.at[:, :, :, lanes] if i < 4 else m.aw5_hbm.at[:, :, :, :, lanes]
+        load(f"aw{i}", src, (m.rw, m.ew, m.jo)[i // 4].at[i % 4], 23 + i)
+    greet = entry_signals(strips)
     for part in range(3):
         off = pl.multiple_of(part * width + c * half, 128)
         load(f"wj{part}", m.wj_hbm.at[:, pl.ds(off, half)], m.wj.at[part], part)
@@ -262,7 +205,48 @@
         spot = pl.ds(n * half, half)
         load(f"we{n}", m.we_hbm.at[:, pl.ds(off, half)], m.we.at[:, spot], 5 + n)
         load(f"wr{n}", m.wr_hbm.at[pl.ds(off, half)], m.wr.at[spot], 5 + chips + n)
-    entry_barrier(strips)
+
+    latents = m.steps.shape[1]
+    classes = m.emb.shape[0]
+    row = lax.broadcasted_iota(jnp.int32, (latents, 1), 0)
+    when = jnp.zeros((latents, 1), F32)
+    label = jnp.zeros((latents, 1), jnp.int32)
+    for i in range(latents):
+        when = jnp.where(row == i, m.steps[0, i].astype(F32), when)
+        label = jnp.where(row == i, m.labels[0, i], label)
+    order = lax.broadcasted_iota(jnp.int32, (latents, half), 1).astype(F32)
+    angles = when * jnp.exp(-math.log(10000.0) * order / half)
+    features = jnp.concatenate([jnp.cos(angles), jnp.sin(angles)], axis=1)
+    onehot = lax.broadcasted_iota(jnp.int32, (latents, classes), 1) == label
+    onehot = jnp.where(onehot, 1.0, 0.0).astype(BF16)
+
+    lane = lax.broadcasted_iota(jnp.int32, (latents, 128), 1)
+    kind = lax.broadcasted_iota(jnp.int32, (latents, 128), 0)
+    line = lax.rem(lane, 16)
+    side = jnp.where(kind == 0, lax.rem(line // 2, 2), lax.rem(line // 3, 2))
+    tile = lax.rem(lane // 16, 4)
+    slots = jnp.zeros((latents, 128), jnp.int32)
+    for i in range(4):
+        for h in range(2):
+            hit = jnp.logical_and(tile == i, side == h)
+            slots = jnp.where(hit, m.owner[0, h, i] + b * latents, slots)
+    loads["emb"].wait()
+    condition = features + dot(onehot, m.emb[...])
+    silu = (condition / (1.0 + jnp.exp(-condition))).astype(BF16)
+    m.cond_all[b] = jnp.concatenate(
+        [condition, jnp.broadcast_to(label.astype(F32), (latents, 128)), slots.astype(F32)], axis=1
+    )
+    bias = m.ab[...].astype(F32).reshape(1, 6 * width)
+    for g, held in enumerate((m.rw, m.ew, m.jo)):
+        for i in range(4):
+            loads[f"aw{4 * g + i}"].wait()
+        weights = jnp.concatenate([held[i].reshape(width, half) for i in range(4)], axis=1)
+        lanes = slice(g * 2 * width, (g + 1) * 2 * width)
+        table = dot(silu, weights) + bias[:, lanes]
+        for h in range(2):
+            mine = row == m.owner[0, h, z]
+            m.mod[h : h + 1, lanes] = jnp.sum(jnp.where(mine, table, 0.0), axis=0, keepdims=True)
+    entry_wait(greet)
 
     m.mk[...] = m.mixer[...].astype(F32)
     ob = m.ob[...].astype(F32).reshape(1, width)
@@ -271,7 +255,6 @@
     for n in range(chips):
         m.hk[n] = m.hidden[:, pl.ds(pl.multiple_of((2 * n + c) * half, 128), half)].astype(F32)
 
-    m.cond_all[b] = m.cond[...]
     for e in range(1, 4):
         start(
             send_to(m.cond_all.at[b], m.cond_all.at[b], m.cond_sem, e, lax.rem(b + e, 4), s)
@@ -465,6 +448,13 @@
         start(send_to(m.ag.at[mine], m.ag.at[mine], m.ag_sem, n, b, sibling))
         m.ai[mine, z] = m.ag[mine, pl.ds(pl.multiple_of(s * 64, 64), 64), :]
 
+    for n in range(chips):
+        loads[f"wr{n}"].wait()
+    send_to(m.tg.at[c], m.tg.at[1 - c], m.pair_sem, 0, b, sibling).wait_recv()
+    chip_tg = m.tg[...].reshape(total, width)
+    for h in range(2):
+        m.big[h] = dot_nt(chip_tg, m.wr[h * width : h * width + width, :]).reshape(m.big.shape[1:])
+
     for n in range(3):
         for d in range(1, strips):
             i = lax.rem(s - d + strips, strips)
@@ -492,13 +482,16 @@
     lax.fori_loop(0, 2 * rows, residual_row, 0, unroll=4)
     start(send_to(m.sc.at[c], m.sc.at[c], m.pair_sem, 1, b, sibling))
 
-    def halo_sends(buffer, sems):
-        up = send_to(buffer.at[1], buffer.at[chip_rows + 1], sems, 0, b, s - 2)
-        down = send_to(buffer.at[chip_rows], buffer.at[0], sems, 1, b, s + 2)
+    def halo_sends(buffer, sems, n):
+        at = slice(None) if n is None else pl.ds(pl.multiple_of(n * half, 128), half)
+        k = 0 if n is None else n
+        first, last = buffer.at[1, :, :, at], buffer.at[chip_rows, :, :, at]
+        up = send_to(first, buffer.at[chip_rows + 1, :, :, at], sems, (0, k), b, s - 2)
+        down = send_to(last, buffer.at[0, :, :, at], sems, (1, k), b, s + 2)
         return up, down
 
-    def start_halo(buffer, sems, upward, downward):
-        up, down = halo_sends(buffer, sems)
+    def start_halo(buffer, sems, upward, downward, n=None):
+        up, down = halo_sends(buffer, sems, n)
 
         @pl.when(jnp.logical_and(z > 0, upward))
         def _():
@@ -508,8 +501,8 @@
         def _():
             down.start()
 
-    def halo_sent(buffer, sems):
-        up, down = halo_sends(buffer, sems)
+    def halo_sent(buffer, sems, n=None):
+        up, down = halo_sends(buffer, sems, n)
 
         @pl.when(z > 0)
         def _():
@@ -519,26 +512,29 @@
         def _():
             down.wait_send()
 
-    def take_halo(buffer, sems):
+    def take_halo(buffer, sems, n=None):
+        at = slice(None) if n is None else pl.ds(n * half, half)
+        k = 0 if n is None else n
+        above, below = buffer.at[0, :, :, at], buffer.at[chip_rows + 1, :, :, at]
+
         @pl.when(z > 0)
         def _():
-            send_to(buffer.at[1], buffer.at[0], sems, 1, b, s - 2).wait_recv()
+            send_to(above, above, sems, (1, k), b, s - 2).wait_recv()
 
         @pl.when(z == 0)
         def _():
-            buffer[0] = jnp.zeros_like(buffer[0])
+            above[...] = jnp.zeros(above.shape, BF16)
 
         @pl.when(z < chips - 1)
         def _():
-            send_to(buffer.at[1], buffer.at[chip_rows + 1], sems, 0, b, s + 2).wait_recv()
+            send_to(below, below, sems, (0, k), b, s + 2).wait_recv()
 
         @pl.when(z == chips - 1)
         def _():
-            buffer[chip_rows + 1] = jnp.zeros_like(buffer[0])
+            below[...] = jnp.zeros(below.shape, BF16)
 
     for n in range(chips):
         loads[f"we{n}"].wait()
-        loads[f"wr{n}"].wait()
     hidden = chips * half
     bias = jnp.concatenate(
         [m.ebf[:, pl.ds(pl.multiple_of((2 * n + c) * half, 128), half)] for n in range(chips)],
@@ -554,16 +550,70 @@
     send_to(m.sc.at[c], m.sc.at[1 - c], m.pair_sem, 1, b, sibling).wait_recv()
     expand(1 - c)
     start_halo(m.ex, m.ex_sem, c == 1, c == 0)
-    send_to(m.tg.at[c], m.tg.at[1 - c], m.pair_sem, 0, b, sibling).wait_recv()
-    chip_tg = m.tg[...].reshape(total, width)
-    for h in range(2):
-        m.big[h] = dot_nt(chip_tg, m.wr[h * width : h * width + width, :]).reshape(m.big.shape[1:])
-
     first_mate, then_mate = (x_mate, y_mate), (y_mate, x_mate)
-    part_rows = width // 8
+    pair_chip = z + 1 - 2 * lax.rem(z, 2)
+    far_chip = lax.rem(z + 2, 4)
+    last_chip = 3 - z
+
+    def block_order(i):
+        high, low = z // 2, lax.rem(z, 2)
+        flip_high, flip_low = 1 - lax.rem(i, 2), 1 - i // 2
+        high = high + flip_high - 2 * high * flip_high
+        low = low + flip_low - 2 * low * flip_low
+        return 2 * high + low
+
+    sub = width // 12
+    upper = pl.ds(0, sub)
+
+    def u_three(k):
+        dest = pair_chip if k < 2 else far_chip
+        src = m.u3.at[1] if k == 2 else m.rw.at[pair_chip if k == 0 else last_chip, :, :, upper]
+        return send_to(src, m.u3.at[k], m.u3_sem, k, b, 2 * dest + c)
+
+    def u_across():
+        u_three(1).wait_recv()
+        for i in range(2):
+            v = m.u3[1, i].astype(F32) + m.rw[far_chip, i, :, upper].astype(F32)
+            m.u3[1, i] = v.astype(BF16)
+        u_three(2).start()
+
+    def u_one(h):
+        at = pl.ds(h * sub // 2, sub // 2)
+        src = m.u0.at[:, 1 - x, at] if h == 0 else m.u0.at[1 - y, :, at]
+        return send_to(src, m.u1.at[h], m.u1_sem, h, first_mate[h], s)
+
+    def u_two(h):
+        src = m.u1.at[h, (1 - y) if h == 0 else (1 - x)]
+        return send_to(src, m.u2.at[h], m.u2_sem, h, then_mate[h], s)
+
+    def u_begin():
+        for k in (0, 2):
+            u_three(k).wait_recv()
+        for i in range(2):
+            v = m.rw[z, i, :, upper].astype(F32) + m.u3[0, i].astype(F32)
+            m.u0[i] = (v + m.u3[2, i].astype(F32)).astype(BF16)
+        for h in range(2):
+            u_one(h).start()
+
+    def u_half():
+        for h in range(2):
+            u_one(h).wait_recv()
+            at = pl.ds(h * sub // 2, sub // 2)
+            kept = m.u0[:, x, at] if h == 0 else m.u0[y, :, at]
+            m.u1[h] = (m.u1[h].astype(F32) + kept.astype(F32)).astype(BF16)
+            u_two(h).start()
+
+    def u_sum():
+        for h in range(2):
+            u_two(h).wait_recv()
+            kept = m.u1[h, y if h == 0 else x].astype(F32)
+            at = pl.ds(h * sub // 2, sub // 2)
+            m.r_all[b, 0, at] = (m.u2[h].astype(F32) + kept).astype(BF16)
+        r_four(0, 0).start()
+        r_four(0, 1).start()
 
     def r_source(n, h, mine):
-        at = pl.ds(h * part_rows, part_rows)
+        at = pl.ds(sub + h * sub, sub)
         if h == 0:
             return m.rw.at[n, :, x if mine else 1 - x, at]
         return m.rw.at[n, y if mine else 1 - y, :, at]
@@ -576,14 +626,30 @@
         return send_to(src, m.r2.at[n, h], m.r2_sem, (n, h), then_mate[h], s)
 
     def r_three(k):
-        z_pair = z + 1 - 2 * lax.rem(z, 2)
-        z_far = lax.rem(z + 2, 4)
-        dest = z_pair if k < 2 else z_far
-        t = (z_pair, 3 - z, z_far)[k]
+        dest = pair_chip if k < 2 else far_chip
+        t = (pair_chip, last_chip, far_chip)[k]
         return send_to(m.r2.at[t], m.r3.at[k], m.r3_sem, k, b, 2 * dest + c)
 
-    def r_four(e):
-        return send_to(m.r_all.at[b], m.r_all.at[b], m.r4_sem, e, lax.rem(b + e, 4), s)
+    def r_four(g, e):
+        spot = m.r_all.at[b, g]
+        return send_to(spot, spot, m.r4_sem, (g, e), (x_mate, y_mate)[e], s)
+
+    def r_relay(g, wait):
+        source, dest = (x_mate, y_mate) if g < 2 else (y_mate, x_mate)
+        spot = m.r_all.at[source, g]
+        copy = send_to(spot, spot, m.r4_sem, (g, 2), dest, s)
+        if wait:
+            copy.wait_send()
+            return
+        send_to(spot, spot, m.r4_sem, (g, 0 if g < 2 else 1), source, s).wait_recv()
+        copy.start()
+
+    def r_arrive(g):
+        source, e = (y_mate, 1) if g < 2 else (x_mate, 0)
+        spot = m.r_all.at[source, g]
+        send_to(spot, spot, m.r4_sem, (g, e), source, s).wait_recv()
+        spot = m.r_all.at[3 - b, g]
+        send_to(spot, spot, m.r4_sem, (g, 2), source, s).wait_recv()
 
     def r_half(n):
         for h in range(2):
@@ -604,8 +670,7 @@
 
     def r_across():
         r_three(1).wait_recv()
-        t = lax.rem(z + 2, 4)
-        m.r2[t] = (m.r2[t].astype(F32) + m.r3[1].astype(F32)).astype(BF16)
+        m.r2[far_chip] = (m.r2[far_chip].astype(F32) + m.r3[1].astype(F32)).astype(BF16)
         r_three(2).start()
 
     def r_sum():
@@ -613,9 +678,10 @@
         for k in (0, 2):
             r_three(k).wait_recv()
             v = v + m.r3[k].astype(F32)
-        m.r_all[b] = v.astype(BF16)
-        for e in range(1, 4):
-            r_four(e).start()
+        m.r_all[b, pl.ds(1, 2)] = v.astype(BF16)
+        for g in (1, 2):
+            r_four(g, 0).start()
+            r_four(g, 1).start()
 
     def c_source(j, h, mine):
         block = m.ew.at[j] if not isinstance(j, int) or j < 4 else m.jo.at[j - 4]
@@ -631,24 +697,80 @@
         src = m.c1.at[j, h, :, 1 - y] if h == 0 else m.c1.at[j, h, :, 1 - x]
         return send_to(src, m.c2.at[j, pl.ds(2 * h, 2)], m.c2_sem, (j, h), then_mate[h], s)
 
-    pair_chip = z + 1 - 2 * lax.rem(z, 2)
-    far_chip = lax.rem(z + 2, 4)
-    last_chip = 3 - z
-
     def c_three(j, k):
         dest = pair_chip if k < 2 else far_chip
         t = (pair_chip, last_chip, far_chip)[k]
         return send_to(m.c2.at[j, t], m.c3.at[j, k], m.c3_sem, (j, k), b, 2 * dest + c)
 
-    def c_four(j, e):
+    def c_copy(j, src, xs, cs, kind, batch, strip):
         return pltpu.make_async_remote_copy(
-            src_ref=m.c_out.at[j],
-            dst_ref=m.c_all.at[j, x, c],
-            send_sem=m.c4_sem[0].at[j, e],
-            recv_sem=m.c4_sem[1].at[j, e, c],
-            device_id=(lax.rem(b + e, 4), 2 * z + y),
+            src_ref=src,
+            dst_ref=m.c_all.at[j, xs, cs],
+            send_sem=m.c4_sem[0].at[j, kind],
+            recv_sem=m.c4_sem[1].at[j, kind, cs],
+            device_id=(batch, strip),
             device_id_type=MESH,
         )
+
+    def c_four(j, kind):
+        return c_copy(j, m.c_out.at[j], x, c, kind, (b, x_mate, y_mate)[kind], 2 * z + y)
+
+    def c_got(j, kind, cs):
+        xs = 1 - x if kind == 1 else x
+        c_copy(j, m.c_out.at[j], xs, cs, kind, b, s).wait_recv()
+
+    def c_passing(j, along_y):
+        xs, dest = (1 - x, y_mate) if along_y else (x, x_mate)
+        return pltpu.make_async_remote_copy(
+            src_ref=m.c_all.at[j, xs],
+            dst_ref=m.c_all.at[j, xs],
+            send_sem=m.c4_sem[0].at[j, 3],
+            recv_sem=m.c4_sem[1].at[j, 3, 0],
+            device_id=(dest, s),
+            device_id_type=MESH,
+        )
+
+    def c_relay(j, along_y):
+        @pl.when((c == y) if along_y else (c != y))
+        def _():
+            for cs in range(2):
+                c_got(j, 1 if along_y else 2, cs)
+            c_passing(j, along_y).start()
+
+    def c_arrive(j, along_y):
+        @pl.when(c == y)
+        def _():
+            c_copy(j, m.c_out.at[j], x, 1 - c, 0, b, sibling).wait_recv()
+            if not along_y:
+                for cs in range(2):
+                    c_got(j, 1, cs)
+
+        @pl.when(c != y)
+        def _():
+            if along_y:
+                for cs in range(2):
+                    c_got(j, 2, cs)
+            spot = m.c_all.at[j, 1 - x]
+            pltpu.make_async_remote_copy(
+                src_ref=spot,
+                dst_ref=spot,
+                send_sem=m.c4_sem[0].at[j, 3],
+                recv_sem=m.c4_sem[1].at[j, 3, 0],
+                device_id=(b, s),
+                device_id_type=MESH,
+            ).wait_recv()
+
+    def c_gone(j, along_y):
+        c_four(j, 1).wait_send()
+        c_four(j, 2).wait_send()
+
+        @pl.when(c != y)
+        def _():
+            c_four(j, 0).wait_send()
+
+        @pl.when((c == y) if along_y else (c != y))
+        def _():
+            c_passing(j, along_y).wait_send()
 
     def c_begin(j):
         for h in range(2):
@@ -689,16 +811,15 @@
         def _():
             m.c_all[j, x, c] = m.c_out[j]
 
-        for e in range(1, 4):
-            c_four(j, e).start()
+        c_four(j, 1).start()
+        c_four(j, 2).start()
 
         @pl.when(c != y)
         def _():
             c_four(j, 0).start()
 
-    take_halo(m.ex, m.ex_sem)
-
-    def activate(n, _):
+    def activate(i, early):
+        n = block_order(i)
         for k in range(3):
             lanes = pl.ds(pl.multiple_of(n * half + k * 128, 128), 128)
             inner = pl.ds(k * 128, 128)
@@ -708,31 +829,57 @@
             def line(r, p):
                 return m.ex[r, p, :, lanes]
 
-            above, here = window(line, 0), window(line, 1)
-            for r in range(chip_rows):
-                below = window(line, r + 2)
-                out = conv((above, here, below), weights, False)
-                for p in range(2):
-                    value, slope = gelu_both(out[p])
-                    rp = 2 * r + p
-                    grad = m.big[n // 2, rp // 16, rp % 16, :, spot]
-                    m.act[rp, :, lanes] = value.astype(BF16)
-                    m.cg[r + 1, p, :, lanes] = (grad * slope).astype(BF16)
-                above, here = here, below
-        full = m.act[:, :, pl.ds(pl.multiple_of(n * half, 128), half)].reshape(total, half)
+            def rows_of(low, high):
+                above, here = window(line, low), window(line, low + 1)
+                for r in range(low, high):
+                    below = window(line, r + 2)
+                    out = conv((above, here, below), weights, False)
+                    for p in range(2):
+                        value, slope = gelu_both(out[p])
+                        rp = 2 * r + p
+                        grad = m.big[n // 2, rp // 16, rp % 16, :, spot]
+                        m.act[rp, :, lanes] = value.astype(BF16)
+                        m.cg[r + 1, p, :, lanes] = (grad * slope).astype(BF16)
+                    above, here = here, below
+
+            if early is None:
+                rows_of(0, chip_rows)
+            elif early:
+                rows_of(1, chip_rows - 1)
+            else:
+                rows_of(0, 1)
+                rows_of(chip_rows - 1, chip_rows)
+
+    def activated(i):
+        n = block_order(i)
+        at = pl.ds(pl.multiple_of(n * half, 128), half)
+        start_halo(m.cg, m.cg_sem, True, True, n)
+        full = m.act[:, :, at].reshape(total, half)
         m.rw[n] = dot_tn(chip_tg, full).astype(BF16).reshape(m.rw.shape[1:])
         for h in range(2):
             r_one(n, h).start()
+
+    activate(0, True)
+    take_halo(m.ex, m.ex_sem)
+    activate(0, False)
+    activated(0)
+    u_three(1).start()
+
+    def next_block(i, _):
+        activate(i, None)
+        activated(i)
         return 0
 
-    lax.fori_loop(0, chips, activate, 0)
-    start_halo(m.cg, m.cg_sem, True, True)
+    lax.fori_loop(1, chips, next_block, 0)
+    u_three(0).start()
     full = m.act[...].reshape(total, hidden)
     m.big[0] = dot(full, m.wr[...]).reshape(m.big.shape[1:])
     b2_copy = send_to(m.big.at[0, 1 - c], m.b2_in, m.pair_sem, 2, b, sibling)
     b2_copy.start()
     m.hkg[...] = jnp.zeros_like(m.hkg)
-    take_halo(m.cg, m.cg_sem)
+    for n in range(chips):
+        take_halo(m.cg, m.cg_sem, n)
+    u_across()
     chip_sc = m.sc[...].reshape(total, width)
 
     def backward(n, _):
@@ -763,7 +910,7 @@
         full = m.act[:, :, pl.ds(pl.multiple_of(n * half, 128), half)].reshape(total, half)
         m.ew[n] = dot_tn(chip_sc, full).astype(BF16).reshape(m.ew.shape[1:])
         c_begin(n)
-        r_half(n)
+        r_half(block_order(n))
         return 0
 
     lax.fori_loop(0, chips, backward, 0)
@@ -852,13 +999,14 @@
 
     pass_on(m.gg, m.gg_sem, m.gg_sem2, 0)
     c_half(0)
+    u_begin()
     c_half(1)
     pass_on(m.gg, m.gg_sem, m.gg_sem2, 1)
     c_half(2)
     pass_on(m.gg, m.gg_sem, m.gg_sem2, 2)
     pass_on(m.gg, m.gg_sem, m.gg_sem2, 3)
+    u_half()
     c_half(3)
-    to_canvases(m.late, m.late_sem, m.late_sem2)
     for n in range(chips):
         r_quarter(n)
     r_spread()
@@ -875,6 +1023,9 @@
     full = jnp.concatenate([m.ag[n] for n in range(6)], axis=-1)
     m.jo[3] = dot_tn(full, columns).astype(BF16).reshape(m.jo.shape[1:])
     c_begin(7)
+    for j in range(3):
+        c_quarter(j)
+        c_spread(j)
 
     tops = lax.broadcasted_iota(jnp.int32, (128, total), 0) < 64
     group = m.mg[...].reshape(total, width)
@@ -900,8 +1051,8 @@
         c_begin(4 + n)
 
     r_across()
-    for j in range(4):
-        c_quarter(j)
+    c_quarter(3)
+    c_spread(3)
 
     b2_copy.wait_send()
     sg_copy.wait_send()
@@ -939,7 +1090,8 @@
         else:
             m.mr[z] = low
 
-    to_sibling(m.late, m.late_sem2, m.late_sem3)
+    for j in range(4):
+        c_across(j)
     sums = m.piece[s].astype(F32)
     for d in range(1, strips):
         send_to(m.piece.at[0], m.piece_in.at[d], m.piece_sem, d, b, s).wait_recv()
@@ -947,12 +1099,16 @@
     m.small[b] = sums.astype(BF16)
     for e in range(1, 4):
         start(send_to(m.small.at[b], m.small.at[b], m.small_sem, e, lax.rem(b + e, 4), s))
-    c_spread(0)
-    c_spread(1)
     c_half(7)
     c_half(4)
     c_half(5)
     c_half(6)
+    to_canvases(m.late, m.late_sem, m.late_sem2)
+    u_sum()
+    r_sum()
+    for j in (7, 4):
+        c_quarter(j)
+        c_spread(j)
 
     for d in range(1, chips):
         i = chip(chips - d)
@@ -961,11 +1117,11 @@
         for p in range(2):
             m.md[r + 1, p] = m.mr[(r % 2) * 2 + p, r // 2]
     start_edges(m.md, m.md_sem)
-    c_spread(2)
-    c_spread(3)
-    c_across(0)
-    c_across(1)
-    r_sum()
+    c_quarter(5)
+    c_spread(5)
+    c_across(7)
+    c_sum(0)
+    c_sum(1)
     for r in range(1, rows - 1):
         for p in range(2):
             m.md[r + 1, p] = m.mr[(r % 2) * 2 + p, r // 2]
@@ -1012,6 +1168,11 @@
 
     mixer_rows(1, rows - 1)
     lax.fori_loop(1, rows - 1, token_row, 0, unroll=3)
+    c_quarter(6)
+    c_spread(6)
+    c_across(4)
+    c_sum(2)
+    c_sum(3)
     top_edge(m.md, m.md_sem)
     mixer_rows(0, 1)
     token_row(0, 0)
@@ -1040,18 +1201,15 @@
         t = lax.rem(s + d, strips)
         start(send_to(m.mpiece.at[t], m.mpiece_in.at[d], m.mpiece_sem, d, b, t))
 
-    for j in (7, 4, 5, 6):
-        c_quarter(j)
-        c_spread(j)
-    c_across(2)
-    c_across(3)
-    c_sum(0)
-    c_sum(1)
+    c_across(5)
+    for g in range(3):
+        r_relay(g, False)
+    for i in range(2):
+        c_relay(i, i % 2 == 0)
+    c_across(6)
+    c_sum(7)
     to_canvases(m.early, m.early_sem, m.early_sem2)
-    c_across(7)
-    c_sum(2)
-    c_sum(3)
-    c_across(4)
+    c_sum(4)
     sums = m.mpiece[s].astype(F32)
     for d in range(1, strips):
         send_to(m.mpiece.at[0], m.mpiece_in.at[d], m.mpiece_sem, d, b, s).wait_recv()
@@ -1059,12 +1217,15 @@
     m.msmall[b] = sums.astype(BF16)
     for e in range(1, 4):
         start(send_to(m.msmall.at[b], m.msmall.at[b], m.msmall_sem, e, lax.rem(b + e, 4), s))
-    c_across(5)
-    c_sum(7)
+    c_sum(5)
+    c_sum(6)
+    for i in range(2, 4):
+        c_relay(i, i % 2 == 0)
+    to_sibling(m.late, m.late_sem2, m.late_sem3)
     to_sibling(m.early, m.early_sem2, m.early_sem3)
-    c_across(6)
-    for j in (4, 5, 6):
-        c_sum(j)
+    j_order = (7, 4, 5, 6)
+    for i in range(4):
+        c_relay(j_order[i], i % 2 == 0)
 
     finals = []
 
@@ -1078,7 +1239,8 @@
         send_to(m.cond_all.at[i], m.cond_all.at[i], m.cond_sem, e, i, s).wait_recv()
         send_to(m.small.at[i], m.small.at[i], m.small_sem, e, i, s).wait_recv()
         send_to(m.msmall.at[i], m.msmall.at[i], m.msmall_sem, e, i, s).wait_recv()
-        send_to(m.r_all.at[i], m.r_all.at[i], m.r4_sem, e, i, s).wait_recv()
+    for g in range(3):
+        r_arrive(g)
     store(m.r_all, m.r_hbm, 15)
     store(m.cond_all, m.cond_hbm, 16)
     store(m.small, m.small_hbm, 17)
@@ -1087,24 +1249,10 @@
     from_sibling(m.early, m.early_sem3)
     store(m.late, m.late_hbm, 19)
     store(m.early, m.early_hbm, 20)
-    for j in range(8):
-        for xs in range(2):
-            for cs in range(2):
-                source = 2 * c + xs
-                e = lax.rem(b - source + 4, 4)
-                local = jnp.logical_and(source == b, cs == c)
-
-                @pl.when(jnp.logical_not(local))
-                def _():
-                    pltpu.make_async_remote_copy(
-                        src_ref=m.c_out.at[j],
-                        dst_ref=m.c_all.at[j, xs, cs],
-                        send_sem=m.c4_sem[0].at[j, e],
-                        recv_sem=m.c4_sem[1].at[j, e, cs],
-                        device_id=(source, 2 * z + cs),
-                        device_id_type=MESH,
-                    ).wait_recv()
-
+    for i in range(4):
+        c_arrive(i, i % 2 == 0)
+    for i in range(4):
+        c_arrive(j_order[i], i % 2 == 0)
     store(m.c_all, m.c_hbm, 21)
     for cp in sent:
         cp.wait_send()
@@ -1112,8 +1260,11 @@
     edges_sent(m.md, m.md_sem)
 
     halo_sent(m.ex, m.ex_sem)
-    halo_sent(m.cg, m.cg_sem)
+    for n in range(chips):
+        halo_sent(m.cg, m.cg_sem, n)
     for h in range(2):
+        u_one(h).wait_send()
+        u_two(h).wait_send()
         for n in range(chips):
             r_one(n, h).wait_send()
             r_two(n, h).wait_send()
@@ -1122,23 +1273,25 @@
             c_two(j, h).wait_send()
     for k in range(3):
         r_three(k).wait_send()
-        r_four(k + 1).wait_send()
+        u_three(k).wait_send()
+        r_four(k, 0).wait_send()
+        r_four(k, 1).wait_send()
+        r_relay(k, True)
         for j in range(8):
             c_three(j, k).wait_send()
-            c_four(j, k + 1).wait_send()
-
-    @pl.when(c != y)
-    def _():
-        for j in range(8):
-            c_four(j, 0).wait_send()
-
+
+    for i in range(4):
+        c_gone(i, i % 2 == 0)
+        c_gone(j_order[i], i % 2 == 0)
     out_copy.wait()
     tg_copy.wait()
     for cp in finals:
         cp.wait()
 
 
-def block(tokens, mod, mixer, owner, cond, ob, eb, hk, rb, wj, wo, we, wr, cot, strips):
+def block(
+    tokens, mixer, owner, steps, labels, emb, aw, ab, ob, eb, hk, rb, wj, wo, we, wr, cot, strips
+):
     rows, cols, width = tokens.shape
     chips = strips // 2
     half = width // 2
@@ -1147,6 +1300,7 @@
     chip_rows = 2 * rows
     part = width // chips // 4
     third = width // 3
+    cond = (steps.shape[1], width + 256)
     shape = jax.ShapeDtypeStruct
     vm = pltpu.VMEM
 
@@ -1154,21 +1308,24 @@
         return pltpu.SemaphoreType.DMA(size)
 
     ins = dict(
-        tok=tokens, mod=mod, mixer=mixer, owner=owner, cond=cond, ob=ob, eb=eb, hidden=hk, rb=rb,
-        wj_hbm=wj, wo_hbm=wo, we_hbm=we, wr_hbm=wr, cot_hbm=cot,
+        tok=tokens, mixer=mixer, owner=owner, steps=steps, labels=labels, ab=ab, ob=ob, eb=eb,
+        hidden=hk, rb=rb, emb_hbm=emb, aw4_hbm=aw.reshape(2, 2, width // 4, 6 * width),
+        aw5_hbm=aw.reshape(chips, 2, 2, part, 6 * width), wj_hbm=wj, wo_hbm=wo, we_hbm=we, wr_hbm=wr, cot_hbm=cot,
     )
     outs = dict(
         out_hbm=shape((rows, cols, width), BF16),
         tg_hbm=shape((rows, cols, width), F32),
-        r_hbm=shape((4, 2, width // 8, half), BF16),
+        r_hbm=shape((4, 3, width // 12, half), BF16),
         c_hbm=shape((8, 2, 2, part, half), BF16),
-        cond_hbm=shape((4,) + cond.shape, F32),
+        cond_hbm=shape((4,) + cond, F32),
         small_hbm=shape((4, 16, half), BF16),
         msmall_hbm=shape((4, 16, 128), BF16),
         late_hbm=shape((4, 2, chips, 16, half), BF16),
         early_hbm=shape((4, 2, chips, 16, third), BF16),
     )
     scratch = dict(
+        emb=vm(emb.shape, BF16),
+        mod=vm((2, 6 * width), F32),
         mk=vm((9, width), F32),
         ebf=vm((1, 2 * chips * half), F32),
         hk=vm((chips, 9, half), F32),
@@ -1177,7 +1334,7 @@
         we=vm((width, chips * half), BF16),
         wr=vm((chips * half, width), BF16),
         cot=vm((rows, cols, width), BF16),
-        cond_all=vm((4,) + cond.shape, F32),
+        cond_all=vm((4,) + cond, F32),
         rowf=vm((rows, width // 128, cols, 128), F32),
         xd=vm((rows, 2, 16, width), BF16),
         fp=vm((rows + 2, 2, 16, width), BF16),
@@ -1215,10 +1372,14 @@
         fg=vm((blocks, 16, width), F32),
         tgo=vm((rows, cols, width), F32),
         rw=vm((chips, 2, 2, width // 4, half), BF16),
-        r1=vm((chips, 2, 2, width // 8, half), BF16),
-        r2=vm((chips, 2, width // 8, half), BF16),
-        r3=vm((3, 2, width // 8, half), BF16),
-        r_all=vm((4, 2, width // 8, half), BF16),
+        r1=vm((chips, 2, 2, width // 12, half), BF16),
+        r2=vm((chips, 2, width // 12, half), BF16),
+        r3=vm((3, 2, width // 12, half), BF16),
+        u3=vm((3, 2, 2, width // 12, half), BF16),
+        u0=vm((2, 2, width // 12, half), BF16),
+        u1=vm((2, 2, width // 24, half), BF16),
+        u2=vm((2, width // 24, half), BF16),
+        r_all=vm((4, 3, width // 12, half), BF16),
         ew=vm((4, chips, 2, 2, part, half), BF16),
         jo=vm((4, chips, 2, 2, part, half), BF16),
         c1=vm((8, 2, 2, 2, part, half), BF16),
@@ -1234,13 +1395,13 @@
         mpiece=vm((strips, 16, 128), BF16),
         mpiece_in=vm((strips, 16, 128), BF16),
         msmall=vm((4, 16, 128), BF16),
-        load_sem=dma(22),
+        load_sem=dma(35),
     )
     pairs = dict(
         cond_sem=(4,), fp_sem=(2,), md_sem=(2,), mg_sem=(chips,), mg_sem2=(chips,),
         gg_sem=(chips,), gg_sem2=(chips,), ai_sem=(3, strips), ag_sem=(3,), pair_sem=(5,),
-        ex_sem=(2,), cg_sem=(2,), mr_sem=(chips,),
-        r1_sem=(chips, 2), r2_sem=(chips, 2), r3_sem=(3,), r4_sem=(4,),
+        ex_sem=(2, 1), cg_sem=(2, chips), mr_sem=(chips,),
+        r1_sem=(chips, 2), r2_sem=(chips, 2), r3_sem=(3,), r4_sem=(3, 3), u3_sem=(3,), u1_sem=(2,), u2_sem=(2,),
         c1_sem=(8, 2), c2_sem=(8, 2), c3_sem=(8, 3),
         late_sem=(chips,), late_sem2=(4,), late_sem3=(1,),
         early_sem=(chips,), early_sem2=(4,), early_sem3=(1,),
@@ -1263,7 +1424,7 @@
         kernel,
         name="block",
         out_shape=tuple(outs.values()),
-        in_specs=[WHOLE] * 3 + [SCALARS] + [WHOLE] * 5 + [LEFT] * 5,
+        in_specs=[WHOLE] * 2 + [SCALARS] * 3 + [WHOLE] * 5 + [LEFT] * 8,
         out_specs=(LEFT,) * len(outs),
         scratch_shapes=shapes,
         compiler_params=pltpu.CompilerParams(
@@ -1283,7 +1444,6 @@
     width = cond_ref.shape[2] - 256
     own = width // strips
     half = width // 2
-    third = width // 3
     loads = [
         (r_in, r_ref),
         (c_in, c_ref),
@@ -1358,34 +1518,28 @@
     slope = sigmoid * (1.0 + condition * (1.0 - sigmoid))
 
     count = 4 * strips * 16
-    row = lax.rem(lax.broadcasted_iota(jnp.int32, (slots, count), 1), 16)
-    index = lax.broadcasted_iota(jnp.int32, (slots, count), 0)
-    hit_late = index == slot_late.astype(jnp.int32)
-    hit_early = index == slot_early.astype(jnp.int32)
-    late = late_ref[...].reshape(count, half)
-    early = early_ref[...].reshape(count, third)
+
+    def by_slot(source, slot, parts, period):
+        groups = parts * (16 // period)
+        index = lax.broadcasted_iota(jnp.int32, (groups * slots, count), 0)
+        row = lax.rem(lax.broadcasted_iota(jnp.int32, (groups * slots, count), 1), 16)
+        group = index // slots
+        mine = jnp.logical_and(
+            row // period == group // parts, lax.rem(row, parts) == lax.rem(group, parts)
+        )
+        mine = jnp.logical_and(mine, lax.rem(index, slots) == slot.astype(jnp.int32))
+        grad = dot(jnp.where(mine, 1.0, 0.0).astype(BF16), source[...].reshape(count, source.shape[-1]))
+        return [grad[k * slots : k * slots + slots] for k in range(groups)]
+
+    pieces = by_slot(early_ref, slot_early, 3, 6) + by_slot(late_ref, slot_late, 2, 4)
+    grad = jnp.concatenate(pieces, axis=1)
+    sums = jnp.sum(grad, axis=0, keepdims=True)
+    low = grad.astype(BF16)
+    ad_ref[...] = dot_tn(silu, low)
     loads[2].wait()
+    silu_grad = dot_nt(low, aw[...])
+    store(ad_ref, ad_out)
     bias = jnp.zeros((1, 6 * own), F32)
-    sums = []
-    silu_grad = jnp.zeros((slots, own), F32)
-    pieces = []
-    for i in range(2):
-        for k in range(3):
-            mine = jnp.logical_or(row == 6 * i + k, row == 6 * i + 3 + k)
-            pieces.append((early, jnp.logical_and(hit_early, mine), i * width + k * third, third))
-    for i in range(4):
-        for k in range(2):
-            mine = jnp.logical_or(row == 4 * i + k, row == 4 * i + 2 + k)
-            pieces.append((late, jnp.logical_and(hit_late, mine), (2 + i) * width + k * half, half))
-    for source, mine, at, size in pieces:
-        chosen = jnp.where(mine, 1.0, 0.0).astype(BF16)
-        grad = dot(chosen, source)
-        sums.append(jnp.sum(grad, axis=0, keepdims=True))
-        low = grad.astype(BF16)
-        ad_ref[:, at : at + size] = dot_tn(silu, low)
-        silu_grad = silu_grad + dot_nt(low, aw[:, at : at + size])
-    store(ad_ref, ad_out)
-    sums = jnp.concatenate(sums, axis=1)
     for t in range(strips):
         bias = jnp.where(s == t, sums[:, t * 6 * own : t * 6 * own + 6 * own], bias)
     ab_ref[...] = bias[0]
@@ -1457,14 +1611,10 @@
 ):
     strips = lax.axis_size("strip")
     owner = tile_owner.transpose(0, 2, 1)
-    mod, cond = conditioning(
-        owner, time_steps, class_labels, class_embedding_matrix.T, adaptive_bias,
-        adaptive_weight,
-    )
     parts = block(
-        tokens[0], mod, mixer_kernel.T, owner, cond, output_bias, expand_bias,
-        hidden_kernel.T, reduce_bias, joint_weight, output_weight, expand_weight, reduce_weight,
-        output_cotangent[0], strips,
+        tokens[0], mixer_kernel.T, owner, time_steps, class_labels, class_embedding_matrix.T,
+        adaptive_weight, adaptive_bias, output_bias, expand_bias, hidden_kernel.T, reduce_bias,
+        joint_weight, output_weight, expand_weight, reduce_weight, output_cotangent[0], strips,
     )
     classes = class_embedding_matrix.shape[1]
     (

time: 144 us -> 131 us (0.910)
  Pallas kernels: 143 us -> 129 us
    pallas_call x1, Pallas kernels: 130 us -> 123 us  [block(): pl.pallas_call(kernel, name='block', out_shape=tuple(outs.values()), in_s...]
    pallas_call x1 -> x0, Pallas kernels: 5.52 us -> none  [conditioning(): pl.pallas_call(condition_kernel, name='conditioning', out_shape=(shape((2...]
    pallas_call x1, Pallas kernels: 8.3 us -> 6.28 us  [final(): pl.pallas_call(final_kernel, name='final', out_shape=(shape(out.shape, BF...]
where the time goes in v1:
time: 131 us; the launch traced here: 130 us
  Pallas kernels  129 us (98%)
    pallas_call x1, Pallas kernels, block(): pl.pallas_call(kernel, name='block', out_shape=tuple(outs.values()), in_s...  123 us
    pallas_call x1, Pallas kernels, final(): pl.pallas_call(final_kernel, name='final', out_shape=(shape(out.shape, BF...  6.28 us

profile of v1, /device:TPU:0, one launch (start us, length us, event | category | flops | bytes accessed | tf_op | source)
XLA Modules:
  0.0 130.1 jit_solution(2163582002381926359)
XLA Ops:
  0.7 123.0 %block.1 = (bf16[8,32,768]{2,1,0:T(8,128)(2,1)}, f32[8,32,768]{2,1,0:T(8,128)}, bf16[4,3,64,384]{3,2,1,0:T(8,128)(2,1)}, bf16[8,2,2,48,384]{4,3,2,1,0:T(8,128)(2...) custom-call(bf16[8,32,768]{2,1,0:T(8,128)(2,1)} %bitcast.15, ...), custom_call_target="tpu_custom_call" | custom-call | tf_op jit(solution)/shard_map/block/pallas_call | solution.py:1423
  123.7 6.3 %final.1 = (bf16[8,32,768]{2,1,0:T(8,128)(2,1)}, f32[8,32,768]{2,1,0:T(8,128)}, f32[96,1000]{1,0:T(8,128)}, f32[96,4608]{1,0:T(8,128)}, f32[576]{0:T(1024)}, /*i...) custom-call(bf16[8,32,768]{2,1,0:T(8,128)(2,1)} %get-tuple-element.3, ...), custom_call_target="tpu_custom_call" | custom-call | tf_op jit(solution)/shard_map/final/pallas_call | solution.py:1566

commit v2 on v1

--- a/solution.py
+++ b/solution.py
@@ -166,6 +166,7 @@
     chip_rows = 2 * rows
     total = strips * 64
     own = width // strips
+    part = width // chips // 4
     s = lax.axis_index("strip")
     b = lax.axis_index("batch")
     z = s // 2
@@ -195,9 +196,9 @@
         src = m.aw4_hbm.at[:, :, :, lanes] if i < 4 else m.aw5_hbm.at[:, :, :, :, lanes]
         load(f"aw{i}", src, (m.rw, m.ew, m.jo)[i // 4].at[i % 4], 23 + i)
     greet = entry_signals(strips)
-    for part in range(3):
-        off = pl.multiple_of(part * width + c * half, 128)
-        load(f"wj{part}", m.wj_hbm.at[:, pl.ds(off, half)], m.wj.at[part], part)
+    for k in range(3):
+        off = pl.multiple_of(k * width + c * half, 128)
+        load(f"wj{k}", m.wj_hbm.at[:, pl.ds(off, half)], m.wj.at[k], k)
     load("cot", m.cot_hbm, m.cot, 3)
     load("wo", m.wo_hbm, m.wo, 4)
     for n in range(chips):
@@ -329,6 +330,37 @@
 
     lax.fori_loop(1, rows - 1, body, 0, unroll=3)
 
+    four = rows // 2
+
+    def inner_rows(g):
+        return pl.ds(1 - g // 2, four - 1)
+
+    def edge_row(g):
+        return pl.ds((g // 2) * (four - 1), 1)
+
+    inner_edge = (inner_rows, edge_row)
+
+    def to_groups(source, target, sems, piece, at):
+        for d in range(1, chips):
+            g = chip(d)
+            rws = at(g)
+            start(
+                send_to(source.at[g, rws], target.at[s, rws], sems, (piece, d), b, 2 * g + c)
+            )
+
+    def pass_on(target, sems, sems2, d, pieces):
+        i = 2 * chip(chips - d) + c
+        if d:
+            for k, at in enumerate(pieces):
+                spot = target.at[i, at(z)]
+                send_to(spot, spot, sems, (k, d), b, i).wait_recv()
+        start(send_to(target.at[i], target.at[i], sems2, d, b, sibling))
+
+    def groups_ready(target, sems2):
+        for d in range(chips):
+            i = 2 * chip(chips - d) + 1 - c
+            send_to(target.at[i], target.at[i], sems2, d, b, sibling).wait_recv()
+
     def mixed_rows(low, high):
         for k in range(width // 128):
             lanes = pl.ds(k * 128, 128)
@@ -349,29 +381,14 @@
             )
 
     mixed_rows(1, rows - 1)
+    to_groups(m.ms, m.mg, m.mg_sem, 0, inner_rows)
     top_edge(m.fp, m.fp_sem)
     mixed_rows(0, 1)
     bottom_edge(m.fp, m.fp_sem)
     mixed_rows(rows - 1, rows)
 
-    def to_groups(source, target, sems, sems2):
-        for d in range(1, chips):
-            g = chip(d)
-            start(send_to(source.at[g], target.at[s], sems, d, b, 2 * g + c))
-        target[s] = source[z]
-
-    def pass_on(target, sems, sems2, d):
-        i = 2 * chip(chips - d) + c
-        if d:
-            send_to(target.at[i], target.at[i], sems, d, b, i).wait_recv()
-        start(send_to(target.at[i], target.at[i], sems2, d, b, sibling))
-
-    def groups_ready(target, sems2):
-        for d in range(chips):
-            i = 2 * chip(chips - d) + 1 - c
-            send_to(target.at[i], target.at[i], sems2, d, b, sibling).wait_recv()
-
-    to_groups(m.ms, m.mg, m.mg_sem, m.mg_sem2)
+    to_groups(m.ms, m.mg, m.mg_sem, 1, edge_row)
+    m.mg[s] = m.ms[z]
 
     m.acc[...] = jnp.zeros_like(m.acc)
     gate2 = block_mod(5)
@@ -391,16 +408,16 @@
     start(send_to(m.tg.at[c], m.tg.at[c], m.pair_sem, 0, b, sibling))
 
     for d in range(chips):
-        pass_on(m.mg, m.mg_sem, m.mg_sem2, d)
+        pass_on(m.mg, m.mg_sem, m.mg_sem2, d, inner_edge)
     groups_ready(m.mg, m.mg_sem2)
-    for part in range(3):
-        loads[f"wj{part}"].wait()
+    for k in range(3):
+        loads[f"wj{k}"].wait()
 
     v = m.mg[...].reshape(total, width)
-    for part in range(3):
-        w = dot(v, m.wj[part]).astype(BF16)
+    for k in range(3):
+        w = dot(v, m.wj[k]).astype(BF16)
         for n in range(3):
-            m.qkv[3 * part + n] = w[:, n * 128 : n * 128 + 128]
+            m.qkv[3 * k + n] = w[:, n * 128 : n * 128 + 128]
 
     where = lax.broadcasted_iota(jnp.int32, (1, total), 1)
     lefts = lax.rem(where, 16) < 8
@@ -482,16 +499,26 @@
     lax.fori_loop(0, 2 * rows, residual_row, 0, unroll=4)
     start(send_to(m.sc.at[c], m.sc.at[c], m.pair_sem, 1, b, sibling))
 
-    def halo_sends(buffer, sems, n):
-        at = slice(None) if n is None else pl.ds(pl.multiple_of(n * half, 128), half)
-        k = 0 if n is None else n
-        first, last = buffer.at[1, :, :, at], buffer.at[chip_rows, :, :, at]
-        up = send_to(first, buffer.at[chip_rows + 1, :, :, at], sems, (0, k), b, s - 2)
-        down = send_to(last, buffer.at[0, :, :, at], sems, (1, k), b, s + 2)
+    def block_order(i, at_chip=None):
+        at_chip = z if at_chip is None else at_chip
+        high, low = at_chip // 2, lax.rem(at_chip, 2)
+        flip_high, flip_low = 1 - lax.rem(i, 2), 1 - i // 2
+        high = high + flip_high - 2 * high * flip_high
+        low = low + flip_low - 2 * low * flip_low
+        return 2 * high + low
+
+    def halo_sends(buffer, sems, up_block, down_block):
+        up_at = pl.ds(pl.multiple_of(up_block * half, 128), half)
+        down_at = pl.ds(pl.multiple_of(down_block * half, 128), half)
+        first, last = buffer.at[1, :, :, up_at], buffer.at[chip_rows, :, :, down_at]
+        above = buffer.at[0, :, :, down_at]
+        below = buffer.at[chip_rows + 1, :, :, up_at]
+        up = send_to(first, below, sems, (0, up_block), b, s - 2)
+        down = send_to(last, above, sems, (1, down_block), b, s + 2)
         return up, down
 
-    def start_halo(buffer, sems, upward, downward, n=None):
-        up, down = halo_sends(buffer, sems, n)
+    def start_halo(buffer, sems, upward, downward, up_block, down_block):
+        up, down = halo_sends(buffer, sems, up_block, down_block)
 
         @pl.when(jnp.logical_and(z > 0, upward))
         def _():
@@ -501,8 +528,8 @@
         def _():
             down.start()
 
-    def halo_sent(buffer, sems, n=None):
-        up, down = halo_sends(buffer, sems, n)
+    def halo_sent(buffer, sems, n):
+        up, down = halo_sends(buffer, sems, n, n)
 
         @pl.when(z > 0)
         def _():
@@ -512,9 +539,9 @@
         def _():
             down.wait_send()
 
-    def take_halo(buffer, sems, n=None):
-        at = slice(None) if n is None else pl.ds(n * half, half)
-        k = 0 if n is None else n
+    def take_halo(buffer, sems, n):
+        at = pl.ds(pl.multiple_of(n * half, 128), half)
+        k = n
         above, below = buffer.at[0, :, :, at], buffer.at[chip_rows + 1, :, :, at]
 
         @pl.when(z > 0)
@@ -546,21 +573,20 @@
         m.ex[pl.ds(1 + core * rows, rows)] = w.astype(BF16).reshape(rows, 2, 16, hidden)
 
     expand(c)
-    start_halo(m.ex, m.ex_sem, c == 0, c == 1)
+    def edges_leave(upward, downward):
+        for i in range(chips):
+            start_halo(
+                m.ex, m.ex_sem, upward, downward, block_order(i, z - 1), block_order(i, z + 1)
+            )
+
+    edges_leave(c == 0, c == 1)
     send_to(m.sc.at[c], m.sc.at[1 - c], m.pair_sem, 1, b, sibling).wait_recv()
     expand(1 - c)
-    start_halo(m.ex, m.ex_sem, c == 1, c == 0)
+    edges_leave(c == 1, c == 0)
     first_mate, then_mate = (x_mate, y_mate), (y_mate, x_mate)
     pair_chip = z + 1 - 2 * lax.rem(z, 2)
     far_chip = lax.rem(z + 2, 4)
     last_chip = 3 - z
-
-    def block_order(i):
-        high, low = z // 2, lax.rem(z, 2)
-        flip_high, flip_low = 1 - lax.rem(i, 2), 1 - i // 2
-        high = high + flip_high - 2 * high * flip_high
-        low = low + flip_low - 2 * low * flip_low
-        return 2 * high + low
 
     sub = width // 12
     upper = pl.ds(0, sub)
@@ -806,7 +832,9 @@
             c_three(j, k).wait_recv()
             v = v + m.c3[j, k].astype(F32)
         m.c_out[j] = v.astype(BF16)
-
+        c_finished(j)
+
+    def c_finished(j):
         @pl.when(c == y)
         def _():
             m.c_all[j, x, c] = m.c_out[j]
@@ -817,6 +845,50 @@
         @pl.when(c != y)
         def _():
             c_four(j, 0).start()
+
+    def v_three(k):
+        dest = pair_chip if k < 2 else far_chip
+        src = m.v3.at[1] if k == 2 else m.ew.at[3, pair_chip if k == 0 else last_chip]
+        return send_to(src, m.v3.at[k], m.v3_sem, k, b, 2 * dest + c)
+
+    def v_across():
+        v_three(1).wait_recv()
+        m.v3[1] = (m.v3[1].astype(F32) + m.ew[3, far_chip].astype(F32)).astype(BF16)
+        v_three(2).start()
+
+    v_rows = (pl.ds(0, 32), pl.ds(32, part - 32))
+
+    def v_one(h):
+        src = m.v0.at[:, 1 - x, v_rows[0]] if h == 0 else m.v0.at[1 - y, :, v_rows[1]]
+        return send_to(src, (m.v1a, m.v1b)[h], m.v1_sem, h, first_mate[h], s)
+
+    def v_two(h):
+        src = m.v1a.at[1 - y] if h == 0 else m.v1b.at[1 - x]
+        return send_to(src, (m.v2a, m.v2b)[h], m.v2_sem, h, then_mate[h], s)
+
+    def v_begin():
+        for k in (0, 2):
+            v_three(k).wait_recv()
+        v = m.ew[3, z].astype(F32) + m.v3[0].astype(F32) + m.v3[2].astype(F32)
+        m.v0[...] = v.astype(BF16)
+        for h in range(2):
+            v_one(h).start()
+
+    def v_half():
+        for h in range(2):
+            v_one(h).wait_recv()
+            held = (m.v1a, m.v1b)[h]
+            kept = m.v0[:, x, v_rows[0]] if h == 0 else m.v0[y, :, v_rows[1]]
+            held[...] = (held[...].astype(F32) + kept.astype(F32)).astype(BF16)
+            v_two(h).start()
+
+    def v_sum():
+        for h in range(2):
+            v_two(h).wait_recv()
+            kept = m.v1a[y] if h == 0 else m.v1b[x]
+            v = (m.v2a, m.v2b)[h][...].astype(F32) + kept.astype(F32)
+            m.c_out[3, v_rows[h]] = v.astype(BF16)
+        c_finished(3)
 
     def activate(i, early):
         n = block_order(i)
@@ -853,17 +925,19 @@
     def activated(i):
         n = block_order(i)
         at = pl.ds(pl.multiple_of(n * half, 128), half)
-        start_halo(m.cg, m.cg_sem, True, True, n)
+        start_halo(m.cg, m.cg_sem, True, True, n, n)
         full = m.act[:, :, at].reshape(total, half)
         m.rw[n] = dot_tn(chip_tg, full).astype(BF16).reshape(m.rw.shape[1:])
         for h in range(2):
             r_one(n, h).start()
 
     activate(0, True)
-    take_halo(m.ex, m.ex_sem)
+    take_halo(m.ex, m.ex_sem, block_order(0))
     activate(0, False)
     activated(0)
     u_three(1).start()
+    for i in range(1, chips):
+        take_halo(m.ex, m.ex_sem, block_order(i))
 
     def next_block(i, _):
         activate(i, None)
@@ -909,11 +983,16 @@
                 m.hkg[n, t : t + 1, inner] = jnp.sum(v, axis=0, keepdims=True)
         full = m.act[:, :, pl.ds(pl.multiple_of(n * half, 128), half)].reshape(total, half)
         m.ew[n] = dot_tn(chip_sc, full).astype(BF16).reshape(m.ew.shape[1:])
-        c_begin(n)
+        @pl.when(n < 3)
+        def _():
+            c_begin(n)
+
         r_half(block_order(n))
         return 0
 
     lax.fori_loop(0, chips, backward, 0)
+    v_three(1).start()
+    v_three(0).start()
     for core in (1 - c, c):
         v = m.act[pl.ds(core * 2 * rows, 2 * rows)].reshape(rows * 32, hidden)
         m.big[1, core] = dot_nt(v, m.we[...]).reshape(m.big.shape[2:])
@@ -945,11 +1024,20 @@
         m.out[r] = joined(m.rowf, r).astype(BF16)
         return 0
 
-    lax.fori_loop(0, rows, finish, 0, unroll=2)
+    def first_half(g):
+        return pl.ds(0, four // 2)
+
+    def second_half(g):
+        return pl.ds(four // 2, four // 2)
+
+    both_halves = (first_half, second_half)
+    for k, at in enumerate(both_halves):
+        lax.fori_loop(k * four, (k + 1) * four, finish, 0, unroll=2)
+        to_groups(m.og, m.gg, m.gg_sem, k, at)
     out_copy = pltpu.make_async_copy(m.out, m.out_hbm, m.load_sem.at[13])
     out_copy.start()
 
-    to_groups(m.og, m.gg, m.gg_sem, m.gg_sem2)
+    m.gg[s] = m.og[z]
 
     pack = []
     for v in (m.acc[3], m.acc[1], m.acc[2], m.acc[5]):
@@ -978,35 +1066,22 @@
         send_to(buffer.at[:, c], buffer.at[:, 1 - c], sems3, 0, b, sibling).wait_recv()
 
     own_sums(m.late, m.late_sem, jnp.concatenate(pack, axis=0))
-    sums_ob = jnp.sum(m.acc[4], axis=0, keepdims=True)
-    sums_rb = jnp.sum(m.acc[0], axis=0, keepdims=True)
-    pad_lanes = jnp.zeros((1, half - own), F32)
-    pad_rows = jnp.zeros((4, half), F32)
-    for t in range(strips):
-        piece = jnp.concatenate(
-            [
-                jnp.where(c == t % 2, m.hkg[t // 2, 0:10], 0.0),
-                jnp.concatenate([sums_ob[:, t * own : t * own + own], pad_lanes], axis=1),
-                jnp.concatenate([sums_rb[:, t * own : t * own + own], pad_lanes], axis=1),
-                pad_rows,
-            ],
-            axis=0,
-        )
-        m.piece[t] = piece.astype(BF16)
-    for d in range(1, strips):
-        t = lax.rem(s + d, strips)
-        start(send_to(m.piece.at[t], m.piece_in.at[d], m.piece_sem, d, b, t))
-
-    pass_on(m.gg, m.gg_sem, m.gg_sem2, 0)
+    for t in range(chips):
+        m.piece[t] = m.hkg[t].astype(BF16)
+    for d in range(1, chips):
+        t = chip(d)
+        start(send_to(m.piece.at[t], m.piece_in.at[d], m.piece_sem, d, b, 2 * t + c))
+
+    pass_on(m.gg, m.gg_sem, m.gg_sem2, 0, both_halves)
     c_half(0)
     u_begin()
     c_half(1)
-    pass_on(m.gg, m.gg_sem, m.gg_sem2, 1)
+    pass_on(m.gg, m.gg_sem, m.gg_sem2, 1, both_halves)
+    v_across()
     c_half(2)
-    pass_on(m.gg, m.gg_sem, m.gg_sem2, 2)
-    pass_on(m.gg, m.gg_sem, m.gg_sem2, 3)
+    pass_on(m.gg, m.gg_sem, m.gg_sem2, 2, both_halves)
+    pass_on(m.gg, m.gg_sem, m.gg_sem2, 3, both_halves)
     u_half()
-    c_half(3)
     for n in range(chips):
         r_quarter(n)
     r_spread()
@@ -1050,9 +1125,8 @@
         m.jo[n] = w.astype(BF16).reshape(m.jo.shape[1:])
         c_begin(4 + n)
 
+    v_begin()
     r_across()
-    c_quarter(3)
-    c_spread(3)
 
     b2_copy.wait_send()
     sg_copy.wait_send()
@@ -1068,18 +1142,17 @@
             )
             for k in range(9)
         ]
-        w = None
-        for part in range(3):
-            v = jnp.concatenate(strip_rows[3 * part : 3 * part + 3], axis=-1)
-            v = dot_nt(v, m.wj[part])
-            w = v if w is None else w + v
+        weights = jnp.concatenate([m.wj[k] for k in range(3)], axis=-1)
+        w = dot_nt(jnp.concatenate(strip_rows, axis=-1), weights)
         m.big[0, core] = w.reshape(m.big.shape[2:])
 
     partial(1 - c)
     start(send_to(m.big.at[0, 1 - c], m.mp_in, m.pair_sem, 4, b, sibling))
     partial(c)
+    c_half(7)
+    for j in range(3):
+        c_across(j)
     send_to(m.big.at[0, c], m.mp_in, m.pair_sem, 4, b, sibling).wait_recv()
-    four = rows // 2
     for d in range(chips):
         i = chip(d)
         at = pl.ds(four * i, four)
@@ -1090,23 +1163,26 @@
         else:
             m.mr[z] = low
 
-    for j in range(4):
-        c_across(j)
-    sums = m.piece[s].astype(F32)
-    for d in range(1, strips):
+    c_half(4)
+    sums = m.piece[z].astype(F32)
+    for d in range(1, chips):
         send_to(m.piece.at[0], m.piece_in.at[d], m.piece_sem, d, b, s).wait_recv()
         sums = sums + m.piece_in[d].astype(F32)
     m.small[b] = sums.astype(BF16)
     for e in range(1, 4):
         start(send_to(m.small.at[b], m.small.at[b], m.small_sem, e, lax.rem(b + e, 4), s))
-    c_half(7)
-    c_half(4)
     c_half(5)
     c_half(6)
+    v_half()
+    u_sum()
     to_canvases(m.late, m.late_sem, m.late_sem2)
-    u_sum()
     r_sum()
     for j in (7, 4):
+        c_quarter(j)
+        c_spread(j)
+    for j in range(3):
+        c_sum(j)
+    for j in (5, 6):
         c_quarter(j)
         c_spread(j)
 
@@ -1117,11 +1193,7 @@
         for p in range(2):
             m.md[r + 1, p] = m.mr[(r % 2) * 2 + p, r // 2]
     start_edges(m.md, m.md_sem)
-    c_quarter(5)
-    c_spread(5)
     c_across(7)
-    c_sum(0)
-    c_sum(1)
     for r in range(1, rows - 1):
         for p in range(2):
             m.md[r + 1, p] = m.mr[(r % 2) * 2 + p, r // 2]
@@ -1168,11 +1240,9 @@
 
     mixer_rows(1, rows - 1)
     lax.fori_loop(1, rows - 1, token_row, 0, unroll=3)
-    c_quarter(6)
-    c_spread(6)
     c_across(4)
-    c_sum(2)
-    c_sum(3)
+    v_sum()
+    c_across(5)
     top_edge(m.md, m.md_sem)
     mixer_rows(0, 1)
     token_row(0, 0)
@@ -1191,7 +1261,8 @@
     pack.append(jnp.zeros((4, third), F32))
     own_sums(m.early, m.early_sem, jnp.concatenate(pack, axis=0))
     mixer_sums = [jnp.sum(m.acc1[t], axis=0, keepdims=True) for t in range(9)]
-    mixer_sums = jnp.concatenate(mixer_sums + [jnp.zeros((7, width), F32)], axis=0)
+    mixer_sums += [jnp.sum(m.acc[k], axis=0, keepdims=True) for k in (4, 0)]
+    mixer_sums = jnp.concatenate(mixer_sums + [jnp.zeros((5, width), F32)], axis=0)
     pad_lanes = jnp.zeros((16, 128 - own), F32)
     for t in range(strips):
         m.mpiece[t] = jnp.concatenate(
@@ -1201,15 +1272,16 @@
         t = lax.rem(s + d, strips)
         start(send_to(m.mpiece.at[t], m.mpiece_in.at[d], m.mpiece_sem, d, b, t))
 
-    c_across(5)
+    c_across(6)
+    c_sum(7)
+    c_sum(4)
     for g in range(3):
         r_relay(g, False)
     for i in range(2):
         c_relay(i, i % 2 == 0)
-    c_across(6)
-    c_sum(7)
+    c_sum(5)
     to_canvases(m.early, m.early_sem, m.early_sem2)
-    c_sum(4)
+    c_sum(6)
     sums = m.mpiece[s].astype(F32)
     for d in range(1, strips):
         send_to(m.mpiece.at[0], m.mpiece_in.at[d], m.mpiece_sem, d, b, s).wait_recv()
@@ -1217,15 +1289,13 @@
     m.msmall[b] = sums.astype(BF16)
     for e in range(1, 4):
         start(send_to(m.msmall.at[b], m.msmall.at[b], m.msmall_sem, e, lax.rem(b + e, 4), s))
-    c_sum(5)
-    c_sum(6)
     for i in range(2, 4):
         c_relay(i, i % 2 == 0)
-    to_sibling(m.late, m.late_sem2, m.late_sem3)
-    to_sibling(m.early, m.early_sem2, m.early_sem3)
     j_order = (7, 4, 5, 6)
     for i in range(4):
         c_relay(j_order[i], i % 2 == 0)
+    to_sibling(m.late, m.late_sem2, m.late_sem3)
+    to_sibling(m.early, m.early_sem2, m.early_sem3)
 
     finals = []
 
@@ -1251,16 +1321,17 @@
     store(m.early, m.early_hbm, 20)
     for i in range(4):
         c_arrive(i, i % 2 == 0)
+    store(m.c_all.at[pl.ds(0, 4)], m.c_hbm.at[pl.ds(0, 4)], 35)
     for i in range(4):
         c_arrive(j_order[i], i % 2 == 0)
-    store(m.c_all, m.c_hbm, 21)
+    store(m.c_all.at[pl.ds(4, 4)], m.c_hbm.at[pl.ds(4, 4)], 21)
     for cp in sent:
         cp.wait_send()
     edges_sent(m.fp, m.fp_sem)
     edges_sent(m.md, m.md_sem)
 
-    halo_sent(m.ex, m.ex_sem)
     for n in range(chips):
+        halo_sent(m.ex, m.ex_sem, n)
         halo_sent(m.cg, m.cg_sem, n)
     for h in range(2):
         u_one(h).wait_send()
@@ -1268,7 +1339,9 @@
         for n in range(chips):
             r_one(n, h).wait_send()
             r_two(n, h).wait_send()
-        for j in range(8):
+        v_one(h).wait_send()
+        v_two(h).wait_send()
+        for j in (0, 1, 2, 4, 5, 6, 7):
             c_one(j, h).wait_send()
             c_two(j, h).wait_send()
     for k in range(3):
@@ -1277,7 +1350,8 @@
         r_four(k, 0).wait_send()
         r_four(k, 1).wait_send()
         r_relay(k, True)
-        for j in range(8):
+        v_three(k).wait_send()
+        for j in (0, 1, 2, 4, 5, 6, 7):
             c_three(j, k).wait_send()
 
     for i in range(4):
@@ -1387,25 +1461,32 @@
         c3=vm((8, 3, part, half), BF16),
         c_out=vm((8, part, half), BF16),
         c_all=vm((8, 2, 2, part, half), BF16),
+        v3=vm((3, 2, 2, part, half), BF16),
+        v0=vm((2, 2, part, half), BF16),
+        v1a=vm((2, 32, half), BF16),
+        v1b=vm((2, part - 32, half), BF16),
+        v2a=vm((32, half), BF16),
+        v2b=vm((part - 32, half), BF16),
         late=vm((4, 2, chips, 16, half), BF16),
         early=vm((4, 2, chips, 16, third), BF16),
-        piece=vm((strips, 16, half), BF16),
-        piece_in=vm((strips, 16, half), BF16),
+        piece=vm((chips, 16, half), BF16),
+        piece_in=vm((chips, 16, half), BF16),
         small=vm((4, 16, half), BF16),
         mpiece=vm((strips, 16, 128), BF16),
         mpiece_in=vm((strips, 16, 128), BF16),
         msmall=vm((4, 16, 128), BF16),
-        load_sem=dma(35),
+        load_sem=dma(36),
     )
     pairs = dict(
-        cond_sem=(4,), fp_sem=(2,), md_sem=(2,), mg_sem=(chips,), mg_sem2=(chips,),
-        gg_sem=(chips,), gg_sem2=(chips,), ai_sem=(3, strips), ag_sem=(3,), pair_sem=(5,),
-        ex_sem=(2, 1), cg_sem=(2, chips), mr_sem=(chips,),
+        cond_sem=(4,), fp_sem=(2,), md_sem=(2,), mg_sem=(2, chips), mg_sem2=(chips,),
+        gg_sem=(2, chips), gg_sem2=(chips,), ai_sem=(3, strips), ag_sem=(3,), pair_sem=(5,),
+        ex_sem=(2, chips), cg_sem=(2, chips), mr_sem=(chips,),
         r1_sem=(chips, 2), r2_sem=(chips, 2), r3_sem=(3,), r4_sem=(3, 3), u3_sem=(3,), u1_sem=(2,), u2_sem=(2,),
+        v3_sem=(3,), v1_sem=(2,), v2_sem=(2,),
         c1_sem=(8, 2), c2_sem=(8, 2), c3_sem=(8, 3),
         late_sem=(chips,), late_sem2=(4,), late_sem3=(1,),
         early_sem=(chips,), early_sem2=(4,), early_sem3=(1,),
-        piece_sem=(strips,), small_sem=(4,), mpiece_sem=(strips,), msmall_sem=(4,),
+        piece_sem=(chips,), small_sem=(4,), mpiece_sem=(strips,), msmall_sem=(4,),
     )
     names = list(ins) + list(outs) + list(scratch)
     shapes = list(scratch.values())
@@ -1468,8 +1549,8 @@
         mixer = mixer + msmall_ref[i].astype(F32)
     hidden_ref[...] = small[0:9]
     eb_ref[...] = small[9]
-    ob_ref[...] = small[10, 0:own]
-    rb_ref[...] = small[11, 0:own]
+    ob_ref[...] = mixer[9, 0:own]
+    rb_ref[...] = mixer[10, 0:own]
     mix_ref[...] = mixer[0:9, 0:own]
 
     n = width // 4

time: 131 us -> 130 us (level)
  no operation moved by 1% of the time
where the time goes in v2:
time: 130 us; the launch traced here: 129 us
  Pallas kernels  128 us (98%)
    pallas_call x1, Pallas kernels, block(): pl.pallas_call(kernel, name='block', out_shape=tuple(outs.values()), in_s...  122 us
    pallas_call x1, Pallas kernels, final(): pl.pallas_call(final_kernel, name='final', out_shape=(shape(out.shape, BF...  6.28 us

profile of v2, /device:TPU:0, one launch (start us, length us, event | category | flops | bytes accessed | tf_op | source)
XLA Modules:
  0.0 129.1 jit_solution(9113050668894890106)
XLA Ops:
  0.7 122.0 %block.1 = (bf16[8,32,768]{2,1,0:T(8,128)(2,1)}, f32[8,32,768]{2,1,0:T(8,128)}, bf16[4,3,64,384]{3,2,1,0:T(8,128)(2,1)}, bf16[8,2,2,48,384]{4,3,2,1,0:T(8,128)(2...) custom-call(bf16[8,32,768]{2,1,0:T(8,128)(2,1)} %bitcast.15, ...), custom_call_target="tpu_custom_call" | custom-call | tf_op jit(solution)/shard_map/block/pallas_call | solution.py:1504
  122.7 6.3 %final.1 = (bf16[8,32,768]{2,1,0:T(8,128)(2,1)}, f32[8,32,768]{2,1,0:T(8,128)}, f32[96,1000]{1,0:T(8,128)}, f32[96,4608]{1,0:T(8,128)}, f32[576]{0:T(1024)}, /*i...) custom-call(bf16[8,32,768]{2,1,0:T(8,128)(2,1)} %get-tuple-element.3, ...), custom_call_target="tpu_custom_call" | custom-call | tf_op jit(solution)/shard_map/final/pallas_call | solution.py:1647

commit v3 on v2

--- a/solution.py
+++ b/solution.py
@@ -231,6 +231,22 @@
         for h in range(2):
             hit = jnp.logical_and(tile == i, side == h)
             slots = jnp.where(hit, m.owner[0, h, i] + b * latents, slots)
+    m.mk[...] = m.mixer[...].astype(F32)
+    ob = m.ob[...].astype(F32).reshape(1, width)
+    rb = m.rb[...].astype(F32).reshape(1, width)
+    m.ebf[...] = m.eb[...].astype(F32).reshape(m.ebf.shape)
+    for n in range(chips):
+        m.hk[n] = m.hidden[:, pl.ds(pl.multiple_of((2 * n + c) * half, 128), half)].astype(F32)
+
+    def normal_row(r, _):
+        spread_columns(m.rowf, r, m.tok[r].astype(F32))
+        for p in range(2):
+            v = every_second(m.rowf, r, p)
+            m.xd[r, p] = v.astype(BF16)
+            m.fg[2 * r + p] = ln_parts(v)[0]
+        return 0
+
+    lax.fori_loop(0, rows, normal_row, 0, unroll=4)
     loads["emb"].wait()
     condition = features + dot(onehot, m.emb[...])
     silu = (condition / (1.0 + jnp.exp(-condition))).astype(BF16)
@@ -249,13 +265,6 @@
             m.mod[h : h + 1, lanes] = jnp.sum(jnp.where(mine, table, 0.0), axis=0, keepdims=True)
     entry_wait(greet)
 
-    m.mk[...] = m.mixer[...].astype(F32)
-    ob = m.ob[...].astype(F32).reshape(1, width)
-    rb = m.rb[...].astype(F32).reshape(1, width)
-    m.ebf[...] = m.eb[...].astype(F32).reshape(m.ebf.shape)
-    for n in range(chips):
-        m.hk[n] = m.hidden[:, pl.ds(pl.multiple_of((2 * n + c) * half, 128), half)].astype(F32)
-
     for e in range(1, 4):
         start(
             send_to(m.cond_all.at[b], m.cond_all.at[b], m.cond_sem, e, lax.rem(b + e, 4), s)
@@ -268,12 +277,8 @@
     shift1 = block_mod(0)
 
     def first_row(r):
-        spread_columns(m.rowf, r, m.tok[r].astype(F32))
         for p in range(2):
-            v = every_second(m.rowf, r, p)
-            m.xd[r, p] = v.astype(BF16)
-            n, _ = ln_parts(v)
-            m.fp[r + 1, p] = (n * scale1 + shift1).astype(BF16)
+            m.fp[r + 1, p] = (m.fg[2 * r + p] * scale1 + shift1).astype(BF16)
 
     def edge_sends(buffer, sems):
         up = send_to(buffer.at[1], buffer.at[rows + 1], sems, 0, b, s - 1)

time: 130 us -> 129 us (level)
  no operation moved by 1% of the time
where the time goes in v3:
time: 129 us; the launch traced here: 128 us
  Pallas kernels  127 us (98%)
    pallas_call x1, Pallas kernels, block(): pl.pallas_call(kernel, name='block', out_shape=tuple(outs.values()), in_s...  121 us
    pallas_call x1, Pallas kernels, final(): pl.pallas_call(final_kernel, name='final', out_shape=(shape(out.shape, BF...  6.29 us

profile of v3, /device:TPU:0, one launch (start us, length us, event | category | flops | bytes accessed | tf_op | source)
XLA Modules:
  0.0 128.3 jit_solution(12540957225099664008)
XLA Ops:
  0.7 121.2 %block.1 = (bf16[8,32,768]{2,1,0:T(8,128)(2,1)}, f32[8,32,768]{2,1,0:T(8,128)}, bf16[4,3,64,384]{3,2,1,0:T(8,128)(2,1)}, bf16[8,2,2,48,384]{4,3,2,1,0:T(8,128)(2...) custom-call(bf16[8,32,768]{2,1,0:T(8,128)(2,1)} %bitcast.15, ...), custom_call_target="tpu_custom_call" | custom-call | tf_op jit(solution)/shard_map/block/pallas_call | solution.py:1509
  121.9 6.3 %final.1 = (bf16[8,32,768]{2,1,0:T(8,128)(2,1)}, f32[8,32,768]{2,1,0:T(8,128)}, f32[96,1000]{1,0:T(8,128)}, f32[96,4608]{1,0:T(8,128)}, f32[576]{0:T(1024)}, /*i...) custom-call(bf16[8,32,768]{2,1,0:T(8,128)(2,1)} %get-tuple-element.3, ...), custom_call_target="tpu_custom_call" | custom-call | tf_op jit(solution)/shard_map/final/pallas_call | solution.py:1652
